TPU v7x, 32 devices: a whole 2x2x4 slice. The times are simulated.
32 devices in a mesh: elem: 8 (over z, x), plane: 4 (over y, core).
Axes of the slice: x: 2, y: 2, z: 4, core: 2. Of those that a mesh axis runs over, the one named last changes fastest.
Arguments:
- velocity: float32 [3, 64, 81, 256], P(None, 'plane', None, 'elem'), may hold values from -4.5 to 4.5
- geometry: float32 [4, 100, 256], P(None, None, 'elem'), may hold values from -3 to 3
- jacobian: float32 [100, 256], P(None, 'elem'), may hold values from 0.5 to 2
- frame_flip: int32 [8], P('elem'), may hold values from 0 to 1
Outputs:
- advection: float32 [3, 64, 81, 256], P(None, 'plane', None, 'elem')
- svv_force: float32 [3, 64, 81, 256], P(None, 'plane', None, 'elem')
All inputs are finite; a program needn't handle non-finite values.
Results may differ from a plain program's by a relative error of at most 0.00005.
Values sent between devices are 32-bit elements; how exact they have to be, the bound alone decides.
A program may use at most 64 MiB of HBM per device.

v0:
```python
import jax
import jax.numpy as jnp
import numpy as np
from jax import lax
from jax.sharding import PartitionSpec as P

P_SIZE = 8
Q = 10
NZ = 64
EY = 8


spanwise_scale = 0.25
svv_cutoff = 4.0
svv_peak = 2.0
sensor_centre = -1.5
sensor_width = 0.6
energy_floor = 1e-06


def from_behind(block, axis, distance):
    devices = range(lax.axis_size(axis))
    route = [(i - distance, i) for i in devices if i - distance in devices]
    return lax.ppermute(block, axis, route)


def modal_basis(top_degree, points):
    legendre = [points * 0.0 + 1.0, points * 1.0]
    for order in range(1, top_degree):
        legendre.append(
            ((2.0 * order + 1.0) * points * legendre[order] - order * legendre[order - 1])
            / (order + 1.0)
        )
    values = np.zeros((points.shape[0], top_degree + 1))
    slopes = np.zeros((points.shape[0], top_degree + 1))
    values[:, 0] = 0.5 * (1.0 - points)
    values[:, 1] = 0.5 * (1.0 + points)
    slopes[:, 0] = -0.5
    slopes[:, 1] = 0.5
    for column in range(2, top_degree + 1):
        values[:, column] = (legendre[column - 2] - points * legendre[column - 1]) / column
        slopes[:, column] = -legendre[column - 1]
    return (values, slopes)


def spectral_tables(top_degree, point_count, planes):
    fine_planes = 3 * planes // 2
    angles_q = np.pi * (np.arange(point_count) + 0.5) / point_count
    points = -np.cos(angles_q)
    series = np.arange(1, point_count // 2 + 1)
    weights = (
        2.0
        / point_count
        * (
            1.0
            - 2.0
            * np.sum(
                np.cos(2.0 * series[None, :] * angles_q[:, None])
                / (4.0 * series[None, :] ** 2 - 1.0),
                axis=1,
            )
        )
    )
    values, slopes = modal_basis(top_degree, points)
    value_table = np.kron(values, values)
    xi_table = np.kron(slopes, values)
    eta_table = np.kron(values, slopes)
    point_weights = np.kron(weights, weights)
    degrees = np.maximum(np.arange(top_degree + 1), 1) * 1.0
    highest = np.maximum(degrees[:, None], degrees[None, :]).reshape(-1)
    tail_mask = (highest > svv_cutoff) * 1.0
    kernel = np.where(
        degrees > svv_cutoff,
        np.exp(-(((top_degree - degrees) / np.maximum(degrees - svv_cutoff, 1.0)) ** 2)),
        0.0,
    )
    per_dir = degrees * (degrees + 1.0) * kernel
    svv_weight = (per_dir[:, None] + per_dir[None, :]).reshape(-1) / (
        top_degree * (top_degree + 1.0)
    )
    angles_z = 2.0 * np.pi * np.arange(fine_planes) / fine_planes
    coef_index = np.arange(planes)
    wavenumber = np.where(coef_index == 1, planes // 2, coef_index // 2)
    cosine_part = (coef_index % 2 == 0) | (coef_index == 1)
    inverse = np.where(
        cosine_part[None, :],
        np.cos(wavenumber[None, :] * angles_z[:, None]),
        np.sin(wavenumber[None, :] * angles_z[:, None]),
    )
    forward = inverse.T * np.where(coef_index == 0, 1.0 / fine_planes, 2.0 / fine_planes)[:, None]
    tables = (
        value_table,
        xi_table,
        eta_table,
        point_weights,
        tail_mask,
        svv_weight,
        inverse,
        forward,
    )
    return tuple((jnp.asarray(table.astype(np.float32)) for table in tables))


def z_slope(coeffs, wavenumbers):
    fields, planes, mode_count, elements = coeffs.shape
    paired = coeffs.reshape(fields, planes // 2, 2, mode_count, elements)
    factor = (spanwise_scale * wavenumbers)[None, :, None, None]
    slope = jnp.stack([factor * paired[:, :, 1], -factor * paired[:, :, 0]], axis=2)
    return slope.reshape(coeffs.shape)


def point_values(coeffs, zcoeffs, geometry, value_table, xi_table, eta_table):
    highest = lax.Precision.HIGHEST
    values = jnp.einsum("qm,fjme->fjqe", value_table, coeffs, precision=highest)
    along_xi = jnp.einsum("qm,fjme->fjqe", xi_table, coeffs, precision=highest)
    along_eta = jnp.einsum("qm,fjme->fjqe", eta_table, coeffs, precision=highest)
    along_z = jnp.einsum("qm,fjme->fjqe", value_table, zcoeffs, precision=highest)
    slope_x = geometry[0] * along_xi + geometry[1] * along_eta
    slope_y = geometry[2] * along_xi + geometry[3] * along_eta
    return jnp.concatenate([values, slope_x, slope_y, along_z], axis=0)


def advect(stacked, inverse, forward):
    highest = lax.Precision.HIGHEST
    physical = jnp.einsum("nj,cjqe->cnqe", inverse, stacked, precision=highest)
    speeds = physical[0:3]
    product = speeds[0] * physical[3:6] + speeds[1] * physical[6:9] + speeds[2] * physical[9:12]
    return jnp.einsum("jn,fnqe->fjqe", forward, product, precision=highest)


def project(nonlinear, jacobian, value_table, point_weights):
    weighted = nonlinear * (jacobian * point_weights[:, None])
    return jnp.einsum("qm,fjqe->fjme", value_table, weighted, precision=lax.Precision.HIGHEST)


def energies(coeffs, tail_mask):
    squares = coeffs * coeffs
    tail_energy = jnp.sum(squares * tail_mask[:, None], axis=(0, 1, 2))
    all_energy = jnp.sum(squares, axis=(0, 1, 2))
    return (tail_energy, all_energy)


def strength_ramp(tail_energy, all_energy):
    log_share = jnp.log((tail_energy + energy_floor) / (all_energy + energy_floor))
    return svv_peak * jax.nn.sigmoid((log_share - sensor_centre) / sensor_width)


def flip_edge(edge_modes):
    count_r = edge_modes.shape[2]
    parity = jnp.where(jnp.arange(2, count_r) % 2 == 0, 1.0, -1.0).astype(jnp.float32)
    parity = parity.reshape((-1,) + (1,) * (edge_modes.ndim - 3))
    swapped = jnp.concatenate(
        [edge_modes[:, :, 1:2], edge_modes[:, :, 0:1], edge_modes[:, :, 2:] * parity], axis=2
    )
    return jnp.flip(swapped, axis=-1)


def to_points(stacked):
    return lax.all_to_all(stacked, "plane", split_axis=3, concat_axis=1, tiled=True)


def to_planes(returned):
    return lax.all_to_all(returned, "plane", split_axis=1, concat_axis=3, tiled=True)


def assemble(weak_rhs, flip_flag):
    fields, planes, mode_count, elements = weak_rhs.shape
    side = P_SIZE + 1
    columns = elements // EY
    modal_grid = weak_rhs.reshape(fields, planes, side, side, columns, EY)
    left_modes = modal_grid[:, :, 0]
    right_modes = modal_grid[:, :, 1]
    flipped = flip_flag == 1

    def canonical(edge_modes):
        return jnp.where(flipped, flip_edge(edge_modes), edge_modes)

    out_right = canonical(right_modes[:, :, :, -1])
    out_left = canonical(left_modes[:, :, :, 0])
    from_left = canonical(from_behind(out_right, "elem", 1))
    from_right = canonical(from_behind(out_left, "elem", -1))
    left_next = jnp.concatenate([left_modes[:, :, :, 1:], from_right[:, :, :, None]], axis=3)
    right_prev = jnp.concatenate([from_left[:, :, :, None], right_modes[:, :, :, :-1]], axis=3)
    modal_grid = jnp.concatenate(
        [
            (left_modes + right_prev)[:, :, None],
            (right_modes + left_next)[:, :, None],
            modal_grid[:, :, 2:],
        ],
        axis=2,
    )
    bottom = modal_grid[:, :, :, 0]
    top = modal_grid[:, :, :, 1]
    no_row = jnp.zeros_like(bottom[..., :1])
    new_bottom = bottom + jnp.concatenate([no_row, top[..., :-1]], axis=-1)
    new_top = top + jnp.concatenate([bottom[..., 1:], no_row], axis=-1)
    modal_grid = jnp.concatenate(
        [new_bottom[:, :, :, None], new_top[:, :, :, None], modal_grid[:, :, :, 2:]], axis=3
    )
    return modal_grid.reshape(weak_rhs.shape)


def body(velocity, geometry, jacobian, frame_flip):
    value_table, xi_table, eta_table, point_weights, tail_mask, svv_weight, inverse, forward = (
        spectral_tables(P_SIZE, Q, NZ)
    )
    planes_here = velocity.shape[1]
    position = lax.axis_index("plane")
    wavenumbers = (position * (planes_here // 2) + jnp.arange(planes_here // 2)).astype(jnp.float32)
    zcoeffs = z_slope(velocity, wavenumbers)
    stacked = point_values(velocity, zcoeffs, geometry, value_table, xi_table, eta_table)
    gathered = to_points(stacked)
    nonlinear = advect(gathered, inverse, forward)
    returned = to_planes(nonlinear)
    weak_rhs = project(returned, jacobian, value_table, point_weights)
    tail_part, all_part = energies(velocity, tail_mask)
    tail_energy, all_energy = lax.psum((tail_part, all_part), "plane")
    strength = strength_ramp(tail_energy, all_energy)
    svv_force = -strength[None, None, None, :] * svv_weight[None, None, :, None] * velocity
    advection = assemble(weak_rhs, frame_flip[0])
    return (advection, svv_force)


def solution(mesh):
    return jax.shard_map(
        body,
        mesh=mesh,
        in_specs=(
            P(None, "plane", None, "elem"),
            P(None, None, "elem"),
            P(None, "elem"),
            P("elem"),
        ),
        out_specs=(P(None, "plane", None, "elem"), P(None, "plane", None, "elem")),
        check_vma=False,
    )
```

profile of v0, /device:TPU:0, one launch (start us, length us, event | category | flops | bytes accessed | tf_op | source)
XLA Modules:
  0.0 115.5 jit_solution(8015466371169938350)
XLA Ops:
  0.6 0.0 copy-start
  0.6 0.8 slice_bitcast_fusion.10
  1.5 0.0 copy-start.4
  1.5 1.9 %fusion.17 = f32[100,3,16,32]{0,3,2,1:T(8,128)S(1)} fusion(f32[100,81,1,1]{0,1,3,2:T(8,128)} %constant.85, f32[3,16,81,32]{2,3,1,0:T(8,128)} %param.12), kind=kOutput, calls=%fused_computation.76 | convolution fusion | flops 149299200 | bytes 1144464 | tf_op jit(solution)/shard_map/qm,fjme->fjqe/dot_general | solution.py:115
  3.4 0.0 copy-start.5
  3.5 1.9 %convolution_bitcast_fusion.4 = f32[3,16,100,32]{2,3,1,0:T(8,128)S(1)} fusion(f32[100,81,1,1]{0,1,3,2:T(8,128)} %constant.84, f32[3,16,81,32]{2,3,1,0:T(8,128)} %param.12), kind=kOutput, calls=%fused_computation.9 | convolution fusion | flops 149299200 | bytes 1144464 | tf_op jit(solution)/shard_map/qm,fjme->fjqe/dot_general | solution.py:114
  5.4 0.0 copy-done
  5.4 0.1 slice_multiply_fusion.5
  5.5 0.1 pad_maximum_fusion.1
  5.6 0.0 copy-done.4
  5.6 0.8 convolution_bitcast_fusion.3
  6.4 0.0 copy-done.5
  6.4 0.8 add_bitcast_fusion.1
  7.3 0.4 pad_maximum_fusion
  7.6 3.5 %copy.35 = f32[12,16,100,32]{2,1,0,3:T(8,128)} copy(f32[12,16,100,32]{2,3,1,0:T(8,128)S(1)} %pad_maximum_fusion) | data formatting | bytes 4915200 | tf_op jit(solution)/shard_map/concatenate | solution.py:120
  11.1 4.8 %all-to-all-start = ((f32[12,16,100,32]{2,1,0,3:T(8,128)}), f32[12,16,100,32]{2,1,0,3:T(8,128)}, u32[]{:S(2)}, u32[]{:S(2)}) async-start(f32[12,16,100,32]{2,1,0,3:T(8,128)} %copy.35), calls=%async_computation | async-start | bytes 6291456 | tf_op jit(solution)/shard_map/all_to_all | solution.py:159
  15.9 0.0 copy-done.11
  15.9 0.3 multiply_reduce_fusion
  16.2 38.1 %all-reduce.2 = (f32[32]{0:T(128)S(1)}, f32[32]{0:T(128)S(1)}) all-reduce(f32[32]{0:T(128)S(1)} %get-tuple-element.7, f32[32]{0:T(128)S(1)} %get-tuple-element.6), channel_id=1, replica_groups=mesh['elem'=8,'plane'=4] {'plane'}, use_global_device_ids=true, to_apply=%region_3.0 | all-reduce | flops 64 | bytes 512 | tf_op jit(solution)/shard_map/psum | solution.py:217
  54.4 0.0 all-to-all-done
  54.4 0.0 copy-start.7
  54.4 2.4 %copy.36 = f32[12,16,100,4,8]{2,1,3,4,0:T(8,128)S(1)} copy(f32[12,16,100,4,8]{2,1,0,4,3:T(8,128)} %bitcast.17) | data formatting | bytes 4915200 | tf_op jit(solution)/shard_map/all_to_all | solution.py:159
  56.8 0.0 copy-start.6
  56.8 4.1 %convolution_bitcast_fusion = f32[12,96,100,8]{2,1,3,0:T(8,128)S(1)} fusion(f32[12,64,100,8]{2,1,3,0:T(8,128)S(1)} %bitcast.113, f32[96,64,1,1]{0,1,3,2:T(8,128)S(1)} %copy-done.7), kind=kOutput, calls=%fused_computation.5 | convolution fusion | flops 707788800 | bytes 6168576 | tf_op jit(solution)/shard_map/nj,cjqe->cnqe/dot_general | solution.py:125
  60.9 0.1 slice_bitcast_fusion.2
  61.0 0.0 copy-start.10
  61.0 0.0 copy-start.8
  61.0 0.0 copy-start.9
  61.0 1.3 %convolution_bitcast_fusion.1 = f32[3,64,100,8]{2,1,3,0:T(8,128)S(1)} fusion(f32[64,96,1,1]{1,0,3,2:T(8,128)S(1)} %copy-done.6, f32[12,96,100,8]{2,1,3,0:T(8,128)S(1)} %convolution_bitcast_fusion, f32[96,100,8]{1,0,2:T(8,128)S(1)} %get-tuple-element.14, f32[96,100,8]{1,0,2:T(8,128)S(1)} %get-tuple-element.13, f32[96,100,8]{1,0,2:T(8,128)S(1)} %get-tuple-element.12), kind=kOutput, calls=%fused_computation.6 | convolution fusion | flops 178099200 | bytes 5365760 | tf_op jit(solution)/shard_map/jn,fnqe->fjqe/dot_general | solution.py:128
  62.3 1.3 %copy.37 = f32[3,64,100,8]{2,3,0,1:T(8,128)} copy(f32[3,64,100,8]{2,1,3,0:T(8,128)S(1)} %convolution_bitcast_fusion.1) | data formatting | bytes 1228800 | tf_op jit(solution)/shard_map/jn,fnqe->fjqe/transpose | solution.py:128
  63.7 3.6 %all-to-all-start.1 = ((f32[3,64,100,8]{2,3,0,1:T(8,128)}), f32[3,64,100,8]{2,3,0,1:T(8,128)S(1)}, u32[]{:S(2)}, u32[]{:S(2)}) async-start(f32[3,64,100,8]{2,3,0,1:T(8,128)} %copy.37), calls=%async_computation.1 | async-start | bytes 1572864 | tf_op jit(solution)/shard_map/all_to_all | solution.py:163
  67.9 0.1 broadcast_multiply_fusion.1
  68.0 0.0 copy-done.8
  68.0 10.9 %all-to-all-done.1 = f32[3,64,100,8]{2,3,0,1:T(8,128)S(1)} async-done(((f32[3,64,100,8]{2,3,0,1:T(8,128)}), f32[3,64,100,8]{2,3,0,1:T(8,128)S(1)}, u32[]{:S(2)}, u32[]{:S(2)}) %all-to-all-start.1) | async-done | bytes 614432 | tf_op jit(solution)/shard_map/all_to_all | solution.py:163
  78.9 0.8 convolution_bitcast_fusion.2
  79.7 3.1 %copy.39 = f32[3,16,81,32]{1,3,2,0:T(8,128)} copy(f32[3,16,81,32]{2,3,1,0:T(8,128)S(1)} %convolution_bitcast_fusion.2) | data formatting | bytes 995328 | tf_op jit(solution)/shard_map/qm,fjqe->fjme/transpose | solution.py:133
  82.8 1.0 copy_bitcast_fusion.1
  83.8 0.0 copy-start.1
  83.9 0.1 slice_multiply_fusion.7
  84.0 1.3 %collective-permute-start.1 = (f32[3,16,9,8]{1,3,2,0:T(8,128)S(1)}, f32[3,16,9,8]{1,3,2,0:T(8,128)S(1)}, u32[]{:S(2)}, u32[]{:S(2)}) collective-permute-start(f32[3,16,9,8]{1,3,2,0:T(8,128)S(1)} %broadcast_select_fusion), channel_id=1, source_target_pairs={{4,0},{8,4},{12,8},{16,12},{20,16},{24,20},{28,24},{5,1},{9,5},{13... | collective-permute-start | bytes 41480 | tf_op jit(solution)/shard_map/ppermute | solution.py:24
  85.3 0.9 broadcast_multiply_fusion
  86.3 2.2 %slice.174 = f32[3,16,7,9,4,8]{1,5,4,3,2,0:T(8,128)S(1)} slice(f32[3,16,9,9,4,8]{1,5,4,3,2,0:T(8,128)} %bitcast.109), slice={[0:3], [0:16], [2:9], [0:9], [0:4], [0:8]} | slice | bytes 774144 | tf_op jit(solution)/shard_map/slice | solution.py:188
  88.4 3.2 %collective-permute-done.1 = f32[3,16,9,8]{1,3,2,0:T(8,128)S(1)} collective-permute-done((f32[3,16,9,8]{1,3,2,0:T(8,128)S(1)}, f32[3,16,9,8]{1,3,2,0:T(8,128)S(1)}, u32[]{:S(2)}, u32[]{:S(2)}) %collective-permute-start.1) | collective-permute-done | bytes 13856 | tf_op jit(solution)/shard_map/ppermute | solution.py:24
  91.6 0.1 slice_multiply_fusion.6
  91.8 1.2 %fusion.12 = (f32[3,16,1,9,4,8]{1,5,4,3,2,0:T(8,128)S(1)}, f32[3,16,1,9,4,8]{1,5,4,3,2,0:T(8,128)S(1)}) fusion(f32[3,16,9,9,4,8]{1,5,4,3,2,0:T(8,128)} %bitcast.110, f32[3,16,1,9,1,8]{1,5,4,3,2,0:T(8,128)S(1)} %select_bitcast_fusion, f32[3,16,9,4,8]{1,4,2,0,3:T(8,128)} %copy-done.1), kind=kLoop, calls=%fused_computation.71 | loop fusion | flops 27648 | bytes 898560 | tf_op jit(solution)/shard_map/slice | solution.py:172
  93.0 0.0 copy-start.2
  93.0 0.8 copy-done.2
  93.8 0.1 slice_multiply_fusion.9
  93.9 0.6 pad_maximum_fusion.2
  94.5 1.6 %rev.13 = f32[3,16,9,8]{1,3,2,0:T(8,128)} reverse(f32[3,16,9,8]{1,3,2,0:T(8,128)} %pad_maximum_fusion.2), dimensions={3} | reverse | bytes 27648 | tf_op jit(solution)/shard_map/jit(_flip)/rev | solution.py:155
  96.1 0.9 broadcast_select_fusion.1
  97.0 4.7 %collective-permute-start = (f32[3,16,9,8]{1,3,2,0:T(8,128)S(1)}, f32[3,16,9,8]{1,3,2,0:T(8,128)S(1)}, u32[]{:S(2)}, u32[]{:S(2)}) collective-permute-start(f32[3,16,9,8]{1,3,2,0:T(8,128)S(1)} %broadcast_select_fusion.1), channel_id=1, source_target_pairs={{0,4},{4,8},{8,12},{12,16},{16,20},{20,24},{24,28},{1,5},{5,9},{9,... | collective-permute-start | bytes 41480 | tf_op jit(solution)/shard_map/ppermute | solution.py:24
  101.7 1.7 %slice_bitcast_fusion.4 = f32[3,16,1,9,3,8]{1,5,3,0,4,2:T(8,128)} fusion(f32[3,16,9,4,8]{1,4,2,0,3:T(8,128)} %bitcast.119), kind=kLoop, calls=%fused_computation.41 | loop fusion | bytes 82944 | tf_op jit(solution)/shard_map/concatenate | solution.py:183
  103.5 0.6 collective-permute-done
  104.1 0.1 slice_multiply_fusion.8
  104.1 0.6 copy-done.3
  104.7 0.7 pad_maximum_fusion.3
  105.3 1.5 %rev.14 = f32[3,16,9,8]{1,3,2,0:T(8,128)} reverse(f32[3,16,9,8]{1,3,2,0:T(8,128)} %pad_maximum_fusion.3), dimensions={3} | reverse | bytes 27648 | tf_op jit(solution)/shard_map/jit(_flip)/rev | solution.py:155
  106.9 0.9 select_bitcast_fusion.1
  107.8 1.2 %maximum_add_fusion = f32[3,16,1,9,4,8]{1,5,3,0,4,2:T(8,128)S(1)} fusion(f32[3,16,1,9,3,8]{1,5,3,0,4,2:T(8,128)} %slice_bitcast_fusion.4, f32[3,16,1,9,1,8]{1,5,3,0,4,2:T(8,128)S(1)} %select_bitcast_fusion.1, f32[3,16,9,9,4,8]{1,5,4,3,2,0:T(8,128)} %bitcast.111), kind=kLoop, calls=%fused_computation.27 | loop fusion | flops 27648 | bytes 843264 | tf_op jit(solution)/shard_map/add | solution.py:186
  109.0 0.1 add_bitcast_fusion.3
  109.2 0.1 add_bitcast_fusion.2
  109.3 2.2 %fusion = f32[3,16,9,9,4,8]{1,5,4,3,2,0:T(8,128)} fusion(f32[3,16,7,9,4,8]{1,5,4,3,2,0:T(8,128)S(1)} %slice.174, f32[3,16,1,9,4,8]{1,5,4,3,2,0:T(8,128)S(1)} %get-tuple-element.16, f32[3,16,9,1,4,8]{1,5,4,3,2,0:T(8,128)S(1)} %add_bitcast_fusion.2, f32[3,16,9,1,4,8]{1,5,4,3,2,0:T(8,128)S(1)} %get-tuple-element.10, f32[3,16,1,9,4,8]{1,5,3,0,4,2:T(8,128)S(1)} %maximum_add_fusion), kind=kLoop, calls=%fused_computation.1 | loop fusion | flops 995328 | bytes 1105920 | tf_op jit(solution)/shard_map/concatenate | solution.py:197
  111.5 4.0 %copy.47 = f32[3,16,81,32]{2,3,1,0:T(8,128)} copy(f32[3,16,81,32]{1,3,2,0:T(8,128)} %bitcast.112) | data formatting | bytes 995328
  (26 shorter events, 0.3 us)
Async XLA Ops:
  0.6 4.8 %copy-start = (f32[3,16,81,32]{2,3,1,0:T(8,128)S(1)}, f32[3,16,81,32]{2,3,1,0:T(8,128)}, u32[]{:S(2)}) copy-start(f32[3,16,81,32]{2,3,1,0:T(8,128)} %param.12) | copy-start | bytes 1492996
  1.5 4.1 %copy-start.4 = (f32[100,81,1,1]{0,1,3,2:T(8,128)S(1)}, f32[100,81,1,1]{0,1,3,2:T(8,128)}, u32[]{:S(2)}) copy-start(f32[100,81,1,1]{0,1,3,2:T(8,128)} %constant.84) | copy-start | bytes 97204
  3.4 3.0 %copy-start.5 = (f32[100,81,1,1]{0,1,3,2:T(8,128)S(1)}, f32[100,81,1,1]{0,1,3,2:T(8,128)}, u32[]{:S(2)}) copy-start(f32[100,81,1,1]{0,1,3,2:T(8,128)} %constant.86) | copy-start | bytes 97204
  11.1 4.8 %copy-start.11 = (f32[81]{0:T(128)S(1)}, f32[81]{0:T(128)}, u32[]{:S(2)}) copy-start(f32[81]{0:T(128)} %constant.75.clone) | copy-start | bytes 976
  11.1 43.2 %all-to-all-start = ((f32[12,16,100,32]{2,1,0,3:T(8,128)}), f32[12,16,100,32]{2,1,0,3:T(8,128)}, u32[]{:S(2)}, u32[]{:S(2)}) async-start(f32[12,16,100,32]{2,1,0,3:T(8,128)} %copy.35), calls=%async_computation | async-start | bytes 6291456 | tf_op jit(solution)/shard_map/all_to_all | solution.py:159
  54.4 2.4 %copy-start.7 = (f32[96,64,1,1]{0,1,3,2:T(8,128)S(1)}, f32[96,64,1,1]{0,1,3,2:T(8,128)}, u32[]{:S(2)}) copy-start(f32[96,64,1,1]{0,1,3,2:T(8,128)} %constant.87) | copy-start | bytes 73732
  56.8 4.2 %copy-start.6 = (f32[64,96,1,1]{1,0,3,2:T(8,128)S(1)}, f32[64,96,1,1]{1,0,3,2:T(8,128)}, u32[]{:S(2)}) copy-start(f32[64,96,1,1]{1,0,3,2:T(8,128)} %constant.88) | copy-start | bytes 73732
  61.0 6.9 %copy-start.10 = (f32[81]{0:T(128)S(1)}, f32[81]{0:T(128)}, u32[]{:S(2)}) copy-start(f32[81]{0:T(128)} %constant.76.clone) | copy-start | bytes 976
  61.0 7.0 %copy-start.8 = (f32[100,32]{0,1:T(8,128)S(1)}, f32[100,32]{0,1:T(8,128)}, u32[]{:S(2)}) copy-start(f32[100,32]{0,1:T(8,128)} %param.14) | copy-start | bytes 38404
  61.0 7.0 %copy-start.9 = (f32[100]{0:T(128)S(1)}, f32[100]{0:T(128)}, u32[]{:S(2)}) copy-start(f32[100]{0:T(128)} %constant.74.clone) | copy-start | bytes 1204
  63.7 15.2 %all-to-all-start.1 = ((f32[3,64,100,8]{2,3,0,1:T(8,128)}), f32[3,64,100,8]{2,3,0,1:T(8,128)S(1)}, u32[]{:S(2)}, u32[]{:S(2)}) async-start(f32[3,64,100,8]{2,3,0,1:T(8,128)} %copy.37), calls=%async_computation.1 | async-start | bytes 1572864 | tf_op jit(solution)/shard_map/all_to_all | solution.py:163
  83.8 1.5 %copy-start.1 = (f32[3,16,9,4,8]{1,4,2,0,3:T(8,128)}, f32[3,16,9,4,8]{1,4,2,0,3:T(8,128)S(1)}, u32[]{:S(2)}) copy-start(f32[3,16,9,4,8]{1,4,2,0,3:T(8,128)S(1)} %copy_bitcast_fusion.1) | copy-start | bytes 165892
  84.0 7.6 %collective-permute-start.1 = (f32[3,16,9,8]{1,3,2,0:T(8,128)S(1)}, f32[3,16,9,8]{1,3,2,0:T(8,128)S(1)}, u32[]{:S(2)}, u32[]{:S(2)}) collective-permute-start(f32[3,16,9,8]{1,3,2,0:T(8,128)S(1)} %broadcast_select_fusion), channel_id=1, source_target_pairs={{4,0},{8,4},{12,8},{16,12},{20,16},{24,20},{28,24},{5,1},{9,5},{13... | collective-permute-start | bytes 41480 | tf_op jit(solution)/shard_map/ppermute | solution.py:24
  93.0 0.8 copy-start.2
  97.0 7.1 %collective-permute-start = (f32[3,16,9,8]{1,3,2,0:T(8,128)S(1)}, f32[3,16,9,8]{1,3,2,0:T(8,128)S(1)}, u32[]{:S(2)}, u32[]{:S(2)}) collective-permute-start(f32[3,16,9,8]{1,3,2,0:T(8,128)S(1)} %broadcast_select_fusion.1), channel_id=1, source_target_pairs={{0,4},{4,8},{8,12},{12,16},{16,20},{20,24},{24,28},{1,5},{5,9},{9,... | collective-permute-start | bytes 41480 | tf_op jit(solution)/shard_map/ppermute | solution.py:24
  104.0 0.6 copy-start.3
where the time goes:
time: 116 us; the launch traced here: 115 us
  blocking collectives  38.1 us (33%)
  local copies, waits for them, and re-layouts  24.7 us (21%)
  waiting for transfers between devices  14.6 us (13%)
  starting transfers between devices  14.4 us (12%)
  matrix products  11.7 us (10%)
  other arithmetic  10.2 us (9%)
  between operations  1.7 us (1%)
    psum x1, blocking collectives, body(): tail_energy, all_energy = lax.psum((tail_part, all_part), 'plane')  38.1 us
    all_to_all x1, waiting for transfers between devices, to_planes(): lax.all_to_all(returned, 'plane', split_axis=1, concat_axis=3, tiled=True)  10.9 us
    ppermute x2, starting transfers between devices, from_behind(): return lax.ppermute(block, axis, route)  6.03 us
    unnamed x26, local copies, waits for them, and re-layouts  5.38 us
    all_to_all x1, starting transfers between devices, to_points(): lax.all_to_all(stacked, 'plane', split_axis=3, concat_axis=1, tiled=True)  4.78 us
    dot_general x1, matrix products, advect(): physical = jnp.einsum('nj,cjqe->cnqe', inverse, stacked, precision=highest)  4.08 us
    ppermute x2, waiting for transfers between devices, from_behind(): return lax.ppermute(block, axis, route)  3.75 us
    all_to_all x1, starting transfers between devices, to_planes(): lax.all_to_all(returned, 'plane', split_axis=1, concat_axis=3, tiled=True)  3.56 us
  transfers between devices with their start and end apart: 4, of which 3 were waited for; matrix products, arithmetic and copies ran while one was open for 5% of the time, Pallas kernels for 0%

commit v1 on v0

--- a/solution.py
+++ b/solution.py
@@ -1,7 +1,11 @@
+import functools
+
 import jax
 import jax.numpy as jnp
 import numpy as np
 from jax import lax
+from jax.experimental import pallas as pl
+from jax.experimental.pallas import tpu as pltpu
 from jax.sharding import PartitionSpec as P
 
 P_SIZE = 8
@@ -88,7 +92,7 @@
         np.sin(wavenumber[None, :] * angles_z[:, None]),
     )
     forward = inverse.T * np.where(coef_index == 0, 1.0 / fine_planes, 2.0 / fine_planes)[:, None]
-    tables = (
+    return (
         value_table,
         xi_table,
         eta_table,
@@ -98,7 +102,6 @@
         inverse,
         forward,
     )
-    return tuple((jnp.asarray(table.astype(np.float32)) for table in tables))
 
 
 def z_slope(coeffs, wavenumbers):
@@ -200,9 +203,419 @@
     return modal_grid.reshape(weak_rhs.shape)
 
 
+MODES = (P_SIZE + 1) * (P_SIZE + 1)
+POINTS = Q * Q
+FINE = 3 * NZ // 2
+WIDE = 256
+LANES = 128
+CHUNKS = 2
+MESH = pl.DeviceIdType.MESH
+
+
+def halves(table):
+    high = table.astype(np.float32).astype(jnp.bfloat16)
+    low = (table - high.astype(np.float64)).astype(jnp.bfloat16)
+    return high, low
+
+
+def kernel_tables():
+    value, xi, eta, weights, tail, svv, inverse, forward = spectral_tables(P_SIZE, Q, NZ)
+    to_point = np.zeros((WIDE, 9 * LANES))
+    to_mode = np.zeros((3 * LANES, WIDE))
+    for field in range(3):
+        rows = slice(field * MODES, (field + 1) * MODES)
+        for kind, table in enumerate((value, xi, eta)):
+            start = (kind * 3 + field) * LANES
+            to_point[rows, start : start + POINTS] = table.T
+        to_mode[field * LANES : field * LANES + POINTS, rows] = value
+    slope = np.zeros((FINE, NZ))
+    for m in range(1, NZ // 2):
+        slope[:, 2 * m + 1] = spanwise_scale * m * inverse[:, 2 * m]
+        slope[:, 2 * m] = -spanwise_scale * m * inverse[:, 2 * m + 1]
+
+    def triple(table):
+        high, low = halves(table)
+        return np.concatenate([high, low, high], axis=1)
+
+    lanes = np.zeros((8, WIDE), np.float32)
+    lanes[0, : 3 * MODES] = np.tile(tail, 3)
+    lanes[1, :MODES] = svv
+    lanes[2, :POINTS] = weights
+    edges = np.zeros((2, 2, 4, WIDE, LANES), np.float32)
+    side = P_SIZE + 1
+    for end in range(2):
+        for slot in range(4):
+            for field in range(3):
+                for r in range(side):
+                    source = field * MODES + end * side
+                    edges[end, 0, slot, source + r, slot * 32 + field * side + r] = 1.0
+                    swapped = 1 - r if r < 2 else r
+                    sign = 1.0 if r < 2 or r % 2 == 0 else -1.0
+                    edges[end, 1, slot, source + swapped, (3 - slot) * 32 + field * side + r] = sign
+    edges = edges.reshape(4, 4 * WIDE, LANES).astype(jnp.bfloat16)
+    return (
+        *halves(to_point),
+        *halves(to_mode),
+        triple(inverse),
+        triple(slope),
+        triple(forward),
+        lanes,
+        edges,
+    )
+
+
+def split(x):
+    high = x.astype(jnp.bfloat16)
+    return high, (x - high.astype(jnp.float32)).astype(jnp.bfloat16)
+
+
+def dot(a, b):
+    return lax.dot_general(a, b, (((1,), (0,)), ((), ())), preferred_element_type=jnp.float32)
+
+
+def dot_t(a, b):
+    return lax.dot_general(a, b, (((1,), (1,)), ((), ())), preferred_element_type=jnp.float32)
+
+
+def dot3(x, high, low):
+    x_high, x_low = split(x)
+    return dot(x_high, high) + dot(x_high, low) + dot(x_low, high)
+
+
+def stacked_halves(x):
+    high, low = split(x)
+    return jnp.concatenate([high, high, low], axis=0)
+
+
+def advance(n_plane, n_elem, flip_ref, vel_ref, geo_ref, jac_ref, ph_ref, pl_ref, mh_ref, ml_ref,
+            inv_ref, slo_ref, fwd_ref, lane_ref, edge_ref, adv_ref, svv_ref,
+            vel_s, pack_s, got_s, weight_s, energy_s, strength_s, point_s, hat_s, back_s, weak_s,
+            edge_out, edge_in, out_s,
+            send_a, recv_a, send_s, recv_s, send_b, recv_b, send_e, recv_e):
+    block = lax.axis_index("elem")
+    me = lax.axis_index("plane")
+    planes = NZ // n_plane
+    rows = EY
+    columns = n_plane
+    elements = rows * columns
+    part = rows // CHUNKS
+    offsets = [2, 1, 3]
+    has_prev = block > 0
+    has_next = block < n_elem - 1
+
+    def peer(offset):
+        return lax.rem(me + offset, n_plane)
+
+    barrier = pltpu.get_barrier_semaphore()
+    for offset in offsets:
+        pl.semaphore_signal(barrier, inc=1, device_id=(block, peer(offset)), device_id_type=MESH)
+
+    @pl.when(has_prev)
+    def _():
+        pl.semaphore_signal(barrier, inc=1, device_id=(block - 1, me), device_id_type=MESH)
+
+    @pl.when(has_next)
+    def _():
+        pl.semaphore_signal(barrier, inc=1, device_id=(block + 1, me), device_id_type=MESH)
+
+    for field in range(3):
+        vel_s[field * planes * elements : (field + 1) * planes * elements, 0:MODES] = vel_ref[field]
+
+    lane = lax.broadcasted_iota(jnp.int32, (planes, LANES), 1)
+    first_cut = LANES - MODES
+
+    def pack(target, element):
+        base = target * rows + element
+        u, v, w = [
+            vel_s[pl.ds(field * planes * elements + base, planes, stride=elements), :]
+            for field in range(3)
+        ]
+        v_turned = pltpu.roll(v, MODES, 1)
+        w_turned = pltpu.roll(w, 2 * MODES - LANES, 1)
+        left = jnp.where(lane < MODES, u, v_turned)
+        right = jnp.where(
+            lane < 2 * MODES - LANES, v_turned, jnp.where(lane < 3 * MODES - LANES, w_turned, 0.0)
+        )
+        return jnp.concatenate([left, right], axis=1)
+
+    def forward_copy(i, chunk):
+        span = pl.ds(chunk * part, part)
+        return pltpu.make_async_remote_copy(
+            src_ref=pack_s.at[i, span],
+            dst_ref=got_s.at[me, span],
+            send_sem=send_a.at[i, chunk],
+            recv_sem=recv_a.at[i, chunk],
+            device_id=(block, peer(offsets[i])),
+            device_id_type=MESH,
+        )
+
+    def back_copy(i, chunk):
+        span = pl.ds(chunk * part, part)
+        return pltpu.make_async_remote_copy(
+            src_ref=back_s.at[peer(offsets[i]), span],
+            dst_ref=weak_s.at[me, span],
+            send_sem=send_b.at[i, chunk],
+            recv_sem=recv_b.at[i, chunk],
+            device_id=(block, peer(offsets[i])),
+            device_id_type=MESH,
+        )
+
+    def strength_copy(i):
+        return pltpu.make_async_remote_copy(
+            src_ref=strength_s.at[n_plane],
+            dst_ref=strength_s.at[me],
+            send_sem=send_s.at[i],
+            recv_sem=recv_s.at[i],
+            device_id=(block, peer(offsets[i])),
+            device_id_type=MESH,
+        )
+
+    def edge_copy(i, target):
+        return pltpu.make_async_remote_copy(
+            src_ref=edge_out.at[i],
+            dst_ref=edge_in.at[i],
+            send_sem=send_e.at[i],
+            recv_sem=recv_e.at[i],
+            device_id=(target, me),
+            device_id_type=MESH,
+        )
+
+    for chunk in range(CHUNKS):
+        for i, offset in enumerate(offsets):
+            target = peer(offset)
+            for element in range(chunk * part, (chunk + 1) * part):
+                pack_s[i, element] = pack(target, element)
+            if chunk == 0 and i == 0:
+                pl.semaphore_wait(
+                    barrier, len(offsets) + has_prev.astype(jnp.int32) + has_next.astype(jnp.int32)
+                )
+            forward_copy(i, chunk).start()
+    for element in range(rows):
+        got_s[me, element] = pack(me, element)
+
+    start = pl.multiple_of(me * rows, 8)
+    area = jac_ref[pl.ds(start, rows), :] * lane_ref[2:3, 0:POINTS]
+    weight_s[...] = jnp.zeros_like(weight_s)
+    for i in range(4):
+        weight_s[i, :, 0:POINTS] = geo_ref[i, pl.ds(start, rows), :] * area
+    weight_s[4, :, 0:POINTS] = area
+
+    for chunk in range(CHUNKS):
+        for i in range(len(offsets)):
+            forward_copy(i, chunk).wait_recv()
+        span = slice(chunk * part, (chunk + 1) * part)
+        x = jnp.concatenate(
+            [got_s[source, element] for element in range(chunk * part, (chunk + 1) * part)
+             for source in range(n_plane)], axis=0)
+        energy_s[span, :] = jnp.sum((x * x).reshape(part, NZ, WIDE), axis=1)
+        point_s[...] = dot3(x, ph_ref[...], pl_ref[...])
+        if chunk == CHUNKS - 1:
+            squares = energy_s[...]
+            tail_energy = jnp.sum(squares * lane_ref[0:1, :], axis=1, keepdims=True)
+            all_energy = jnp.sum(squares, axis=1, keepdims=True)
+            log_share = jnp.log((tail_energy + energy_floor) / (all_energy + energy_floor))
+            ramp = (log_share - sensor_centre) / sensor_width
+            strength = svv_peak / (1.0 + jnp.exp(-ramp))
+            strength_s[n_plane] = jnp.broadcast_to(strength, (rows, LANES))
+            strength_s[me] = jnp.broadcast_to(strength, (rows, LANES))
+            for i in range(len(offsets)):
+                strength_copy(i).start()
+
+        for local in range(part):
+            element = chunk * part + local
+            here = slice(local * NZ, (local + 1) * NZ)
+            u = point_s[here, 0:LANES]
+            v = point_s[here, LANES : 2 * LANES]
+            w = point_s[here, 2 * LANES : 3 * LANES]
+            g = [weight_s[i, element : element + 1, :] for i in range(5)]
+            carriers = jnp.concatenate([g[0] * u + g[2] * v, g[1] * u + g[3] * v, g[4] * w], axis=1)
+            speeds = dot(inv_ref[...], stacked_halves(carriers))
+            slopes = dot(inv_ref[...], stacked_halves(point_s[here, 3 * LANES :]))
+            along_z = dot(slo_ref[...], stacked_halves(point_s[here, 0 : 3 * LANES]))
+            product = jnp.concatenate(
+                [
+                    speeds[:, 0:LANES] * slopes[:, f * LANES : (f + 1) * LANES]
+                    + speeds[:, LANES : 2 * LANES] * slopes[:, (3 + f) * LANES : (4 + f) * LANES]
+                    + speeds[:, 2 * LANES :] * along_z[:, f * LANES : (f + 1) * LANES]
+                    for f in range(3)
+                ],
+                axis=1,
+            )
+            hat_s[here, :] = dot(fwd_ref[...], stacked_halves(product))
+        weak = dot3(hat_s[...], mh_ref[...], ml_ref[...])
+        for local in range(part):
+            for k in range(n_plane):
+                first = local * NZ + k * planes
+                back_s[k, chunk * part + local] = weak[first : first + planes]
+        for i in range(len(offsets)):
+            back_copy(i, chunk).start()
+        for local in range(part):
+            weak_s[me, chunk * part + local] = back_s[me, chunk * part + local]
+
+    for i in range(len(offsets)):
+        strength_copy(i).wait_recv()
+    for column in range(columns):
+        factor = -strength_s[column] * lane_ref[1:2, 0:LANES]
+        for field in range(3):
+            for j in range(planes):
+                at = slice(j * elements + column * rows, j * elements + (column + 1) * rows)
+                svv_ref[field, at, :] = vel_ref[field, at, :] * factor[:, 0:MODES]
+
+    for chunk in range(CHUNKS):
+        for i in range(len(offsets)):
+            back_copy(i, chunk).wait_recv()
+
+    flipped = flip_ref[0] == 1
+    turn = jnp.where(flipped, 1, 0)
+    for i, column in ((0, 0), (1, columns - 1)):
+        table = edge_ref[2 * i + turn]
+        tiles = []
+        for half in range(2):
+            picked = jnp.concatenate([weak_s[column, 4 * half + s] for s in range(4)], axis=1)
+            high, low = split(picked)
+            tiles.append(dot(high, table) + dot(low, table))
+        edge_out[i, 0] = jnp.where(flipped, tiles[1], tiles[0])
+        edge_out[i, 1] = jnp.where(flipped, tiles[0], tiles[1])
+
+    @pl.when(has_prev)
+    def _():
+        edge_copy(0, block - 1).start()
+
+    @pl.when(has_next)
+    def _():
+        edge_copy(1, block + 1).start()
+
+    wide = lax.broadcasted_iota(jnp.int32, (planes, WIDE), 1)
+    side = P_SIZE + 1
+    inside = wide < 3 * MODES
+    is_left = inside & (lax.rem(wide, MODES) < side)
+    is_right = inside & (lax.rem(wide, MODES) >= side) & (lax.rem(wide, MODES) < 2 * side)
+    is_bottom = inside & (lax.rem(wide, side) == 0)
+    is_top = inside & (lax.rem(wide, side) == 1)
+
+    for row in range(rows):
+        strip = [weak_s[column, row] for column in range(columns)]
+        for column in range(columns):
+            total = strip[column]
+            if column > 0:
+                total = total + jnp.where(is_left, pltpu.roll(strip[column - 1], WIDE - side, 1), 0.0)
+            if column < columns - 1:
+                total = total + jnp.where(is_right, pltpu.roll(strip[column + 1], side, 1), 0.0)
+            got_s[column, row] = total
+
+    @pl.when(has_next)
+    def _():
+        edge_copy(0, block + 1).wait_recv()
+
+    @pl.when(block == n_elem - 1)
+    def _():
+        edge_in[0] = jnp.zeros((2, planes, LANES), jnp.float32)
+
+    @pl.when(has_prev)
+    def _():
+        edge_copy(1, block - 1).wait_recv()
+
+    @pl.when(block == 0)
+    def _():
+        edge_in[1] = jnp.zeros((2, planes, LANES), jnp.float32)
+
+    for i, column in ((1, 0), (0, columns - 1)):
+        table = edge_ref[2 * (1 - i) + turn]
+        for half in range(2):
+            tile = jnp.where(flipped, edge_in[i, 1 - half], edge_in[i, half])
+            high, low = split(tile)
+            spread = dot_t(high, table) + dot_t(low, table)
+            for s in range(4):
+                got_s[column, 4 * half + s] += spread[:, s * WIDE : (s + 1) * WIDE]
+
+    for column in range(columns):
+        strip = [got_s[column, row] for row in range(rows)]
+        for row in range(rows):
+            total = strip[row]
+            if row > 0:
+                total = total + jnp.where(is_bottom, pltpu.roll(strip[row - 1], WIDE - 1, 1), 0.0)
+            if row < rows - 1:
+                total = total + jnp.where(is_top, pltpu.roll(strip[row + 1], 1, 1), 0.0)
+            fields = (
+                total[:, 0:LANES],
+                pltpu.roll(total, WIDE - MODES, 1)[:, 0:LANES],
+                pltpu.roll(total, WIDE - 2 * MODES, 1)[:, 0:LANES],
+            )
+            for field in range(3):
+                base = field * planes * elements + column * rows + row
+                out_s[pl.ds(base, planes, stride=elements), :] = fields[field]
+    for field in range(3):
+        adv_ref[field] = out_s[field * planes * elements : (field + 1) * planes * elements, 0:MODES]
+
+    for i in range(len(offsets)):
+        strength_copy(i).wait_send()
+        for chunk in range(CHUNKS):
+            forward_copy(i, chunk).wait_send()
+            back_copy(i, chunk).wait_send()
+
+    @pl.when(has_prev)
+    def _():
+        edge_copy(0, block - 1).wait_send()
+
+    @pl.when(has_next)
+    def _():
+        edge_copy(1, block + 1).wait_send()
+
+
+def kernel_body(n_plane, n_elem, velocity, geometry, jacobian, frame_flip):
+    planes, elements = velocity.shape[1], velocity.shape[3]
+    tables = [jnp.asarray(table) for table in kernel_tables()]
+    vel = velocity.transpose(0, 1, 3, 2).reshape(3, planes * elements, MODES)
+    geo = geometry.transpose(0, 2, 1)
+    jac = jacobian.transpose(1, 0)
+    whole = pl.BlockSpec(memory_space=pltpu.VMEM)
+    part = EY // CHUNKS
+    flat = jax.ShapeDtypeStruct((3, planes * elements, MODES), jnp.float32)
+    f32 = jnp.float32
+    dma = pltpu.SemaphoreType.DMA
+    others = n_plane - 1
+    advection, svv = pl.pallas_call(
+        functools.partial(advance, n_plane, n_elem),
+        out_shape=(flat, flat),
+        in_specs=[pl.BlockSpec(memory_space=pltpu.SMEM)] + [whole] * (3 + len(tables)),
+        out_specs=(whole, whole),
+        scratch_shapes=[
+            pltpu.VMEM((3 * planes * elements, LANES), f32),
+            pltpu.VMEM((others, EY, planes, WIDE), f32),
+            pltpu.VMEM((n_plane, EY, planes, WIDE), f32),
+            pltpu.VMEM((5, EY, LANES), f32),
+            pltpu.VMEM((EY, WIDE), f32),
+            pltpu.VMEM((n_plane + 1, EY, LANES), f32),
+            pltpu.VMEM((part * NZ, 9 * LANES), f32),
+            pltpu.VMEM((part * NZ, 3 * LANES), f32),
+            pltpu.VMEM((n_plane, EY, planes, WIDE), f32),
+            pltpu.VMEM((n_plane, EY, planes, WIDE), f32),
+            pltpu.VMEM((2, 2, planes, LANES), f32),
+            pltpu.VMEM((2, 2, planes, LANES), f32),
+            pltpu.VMEM((3 * planes * elements, LANES), f32),
+            dma((others, CHUNKS)),
+            dma((others, CHUNKS)),
+            dma((others,)),
+            dma((others,)),
+            dma((others, CHUNKS)),
+            dma((others, CHUNKS)),
+            dma((2,)),
+            dma((2,)),
+        ],
+        compiler_params=pltpu.CompilerParams(
+            collective_id=0, has_side_effects=True, vmem_limit_bytes=40 * 1024 * 1024
+        ),
+    )(frame_flip, vel, geo, jac, *tables)
+
+    def restore(x):
+        return x.reshape(3, planes, elements, MODES).transpose(0, 1, 3, 2)
+
+    return restore(advection), restore(svv)
+
+
 def body(velocity, geometry, jacobian, frame_flip):
     value_table, xi_table, eta_table, point_weights, tail_mask, svv_weight, inverse, forward = (
-        spectral_tables(P_SIZE, Q, NZ)
+        jnp.asarray(table.astype(np.float32)) for table in spectral_tables(P_SIZE, Q, NZ)
     )
     planes_here = velocity.shape[1]
     position = lax.axis_index("plane")
@@ -222,8 +635,10 @@
 
 
 def solution(mesh):
+    n_plane, n_elem = mesh.shape["plane"], mesh.shape["elem"]
+    fits = n_plane == 4 and (NZ // n_plane) % 16 == 0
     return jax.shard_map(
-        body,
+        functools.partial(kernel_body, n_plane, n_elem) if fits else body,
         mesh=mesh,
         in_specs=(
             P(None, "plane", None, "elem"),

time: 116 us -> 37.8 us (0.33)
  blocking collectives: 38.1 us -> 0 us
  Pallas kernels: 0 us -> 23.7 us
  waiting for transfers between devices: 14.6 us -> 0 us
  starting transfers between devices: 14.4 us -> 0 us
  local copies, waits for them, and re-layouts: 24.7 us -> 12.1 us
  matrix products: 11.7 us -> 0 us
  other arithmetic: 10.2 us -> 0 us
    psum x1 -> x0, blocking collectives: 38.1 us -> none  [body(): tail_energy, all_energy = lax.psum((tail_part, all_part), 'plane')]
    pallas_call x0 -> x1, Pallas kernels: none -> 23.7 us  [kernel_body(): pl.pallas_call(functools.partial(advance, n_plane, n_elem), out_shape=(fl...]
    dot_general x7 -> x0, matrix products: 11.7 us -> none  [the longest x1 4.08 us: advect(): physical = jnp.einsum('nj,cjqe->cnqe', inverse, stacked, precision=highest)]
    all_to_all x2 -> x0, waiting for transfers between devices: 10.9 us -> none  [the longest x1 10.9 us: to_planes(): lax.all_to_all(returned, 'plane', split_axis=1, concat_axis=3, tiled=True)]
    all_to_all x2 -> x0, starting transfers between devices: 8.34 us -> none  [the longest x1 4.78 us: to_points(): lax.all_to_all(stacked, 'plane', split_axis=3, concat_axis=1, tiled=True)]
    unnamed x26, local copies, waits for them, and re-layouts: 5.38 us -> 12.1 us
    ppermute x2 -> x0, starting transfers between devices: 6.03 us -> none  [from_behind(): return lax.ppermute(block, axis, route)]
    concatenate x2 -> x0, local copies, waits for them, and re-layouts: 5.21 us -> none  [the longest x1 3.5 us: point_values(): return jnp.concatenate([values, slope_x, slope_y, along_z], axis=0)]
  transfers between devices with their start and end apart: 4 -> 0, of which waited for: 3 -> 0; matrix products, arithmetic and copies ran while one was open for 5% -> 0% of each run, Pallas kernels for 0% -> 0%
where the time goes in v1:
time: 37.8 us; the launch traced here: 37.1 us
  Pallas kernels  23.7 us (63%)
  local copies, waits for them, and re-layouts  12.1 us (32%)
  between operations  1.32 us (3%)
    pallas_call x1, Pallas kernels, kernel_body(): pl.pallas_call(functools.partial(advance, n_plane, n_elem), out_shape=(fl...  23.7 us
    unnamed x26, local copies, waits for them, and re-layouts  12.1 us

profile of v1, /device:TPU:0, one launch (start us, length us, event | category | flops | bytes accessed | tf_op | source)
XLA Modules:
  0.0 37.1 jit_solution(2641460689241149918)
XLA Ops:
  0.6 0.0 copy-start.11
  1.3 0.0 copy-done.11
  1.3 0.0 copy-start
  1.3 1.2 %copy-done = bf16[4,1024,128]{2,1,0:T(8,128)(2,1)S(1)} copy-done((bf16[4,1024,128]{2,1,0:T(8,128)(2,1)S(1)}, bf16[4,1024,128]{2,1,0:T(8,128)(2,1)}, u32[]{:S(2)}) %copy-start) | copy-done | bytes 1048600
  2.6 0.0 copy-start.1
  2.6 1.1 %copy-done.1 = f32[3,16,81,32]{2,3,1,0:T(8,128)S(1)} copy-done((f32[3,16,81,32]{2,3,1,0:T(8,128)S(1)}, f32[3,16,81,32]{2,3,1,0:T(8,128)}, u32[]{:S(2)}) %copy-start.1) | copy-done | bytes 497688
  3.7 0.0 copy-start.2
  3.7 1.1 %copy-done.2 = bf16[256,1152]{1,0:T(8,128)(2,1)S(1)} copy-done((bf16[256,1152]{1,0:T(8,128)(2,1)S(1)}, bf16[256,1152]{1,0:T(8,128)(2,1)}, u32[]{:S(2)}) %copy-start.2) | copy-done | bytes 589848
  4.8 0.0 copy-start.3
  4.8 1.1 %copy-done.3 = bf16[256,1152]{1,0:T(8,128)(2,1)S(1)} copy-done((bf16[256,1152]{1,0:T(8,128)(2,1)S(1)}, bf16[256,1152]{1,0:T(8,128)(2,1)}, u32[]{:S(2)}) %copy-start.3) | copy-done | bytes 589848
  5.8 0.0 copy-start.4
  5.8 0.9 %copy-done.4 = bf16[384,256]{1,0:T(8,128)(2,1)S(1)} copy-done((bf16[384,256]{1,0:T(8,128)(2,1)S(1)}, bf16[384,256]{1,0:T(8,128)(2,1)}, u32[]{:S(2)}) %copy-start.4) | copy-done | bytes 196632
  6.7 0.0 copy-start.5
  6.7 0.9 %copy-done.5 = bf16[384,256]{1,0:T(8,128)(2,1)S(1)} copy-done((bf16[384,256]{1,0:T(8,128)(2,1)S(1)}, bf16[384,256]{1,0:T(8,128)(2,1)}, u32[]{:S(2)}) %copy-start.5) | copy-done | bytes 196632
  7.7 0.0 copy-start.6
  7.7 0.8 %copy-done.6 = f32[4,100,32]{1,2,0:T(8,128)S(1)} copy-done((f32[4,100,32]{1,2,0:T(8,128)S(1)}, f32[4,100,32]{1,2,0:T(8,128)}, u32[]{:S(2)}) %copy-start.6) | copy-done | bytes 51224
  8.5 0.0 copy-start.7
  8.5 0.8 %copy-done.7 = bf16[64,288]{1,0:T(8,128)(2,1)S(1)} copy-done((bf16[64,288]{1,0:T(8,128)(2,1)S(1)}, bf16[64,288]{1,0:T(8,128)(2,1)}, u32[]{:S(2)}) %copy-start.7) | copy-done | bytes 36888
  9.3 0.0 copy-start.8
  9.3 0.8 %copy-done.8 = bf16[96,192]{1,0:T(8,128)(2,1)S(1)} copy-done((bf16[96,192]{1,0:T(8,128)(2,1)S(1)}, bf16[96,192]{1,0:T(8,128)(2,1)}, u32[]{:S(2)}) %copy-start.8) | copy-done | bytes 36888
  10.1 0.0 copy-start.9
  10.1 0.8 %copy-done.9 = bf16[96,192]{1,0:T(8,128)(2,1)S(1)} copy-done((bf16[96,192]{1,0:T(8,128)(2,1)S(1)}, bf16[96,192]{1,0:T(8,128)(2,1)}, u32[]{:S(2)}) %copy-start.9) | copy-done | bytes 36888
  10.9 0.0 copy-start.10
  10.9 0.7 %copy-done.10 = f32[100,32]{0,1:T(8,128)S(1)} copy-done((f32[100,32]{0,1:T(8,128)S(1)}, f32[100,32]{0,1:T(8,128)}, u32[]{:S(2)}) %copy-start.10) | copy-done | bytes 12824
  11.6 23.7 %shard_map.140 = (f32[3,512,81]{2,1,0:T(8,128)S(1)}, f32[3,512,81]{2,1,0:T(8,128)S(1)}) custom-call(s32[1]{0:T(128)S(6)} %copy.17.flip_ref, f32[3,512,81]{2,1,0:T(8,128)S(1)} %bitcast.13, f32[4,32,100]{2,1,0:T(8,128)S(1)} %bitcast.14, f32[32,100]{1,0:T(8,128)S(1)} %bitcast.15, bf16[256,1152]{1,0:T(8,128)(2,1)S(1)} %copy-done.3, ...), custom_call_target="tpu_custom_call" | custom-call | tf_op jit(solution)/shard_map/pallas_call | solution.py:577
  35.4 0.9 %copy.18 = f32[3,16,81,32]{2,3,1,0:T(8,128)} copy(f32[3,16,81,32]{2,3,1,0:T(8,128)S(1)} %bitcast.12) | data formatting | bytes 995328
  36.2 0.9 %copy.19 = f32[3,16,81,32]{2,3,1,0:T(8,128)} copy(f32[3,16,81,32]{2,3,1,0:T(8,128)S(1)} %bitcast.11) | data formatting | bytes 995328
Async XLA Ops:
  0.6 0.7 %copy-start.11 = (f32[8,256]{1,0:T(8,128)S(1)}, f32[8,256]{1,0:T(8,128)}, u32[]{:S(2)}) copy-start(f32[8,256]{1,0:T(8,128)} %constant.25.clone.lane_ref) | copy-start | bytes 24580
  1.3 1.2 %copy-start = (bf16[4,1024,128]{2,1,0:T(8,128)(2,1)S(1)}, bf16[4,1024,128]{2,1,0:T(8,128)(2,1)}, u32[]{:S(2)}) copy-start(bf16[4,1024,128]{2,1,0:T(8,128)(2,1)} %constant.26.clone.edge_ref) | copy-start | bytes 3145732
  2.6 1.1 %copy-start.1 = (f32[3,16,81,32]{2,3,1,0:T(8,128)S(1)}, f32[3,16,81,32]{2,3,1,0:T(8,128)}, u32[]{:S(2)}) copy-start(f32[3,16,81,32]{2,3,1,0:T(8,128)} %param.13) | copy-start | bytes 1492996
  3.7 1.1 %copy-start.2 = (bf16[256,1152]{1,0:T(8,128)(2,1)S(1)}, bf16[256,1152]{1,0:T(8,128)(2,1)}, u32[]{:S(2)}) copy-start(bf16[256,1152]{1,0:T(8,128)(2,1)} %constant.19.clone.pl_ref) | copy-start | bytes 1769476
  4.8 1.1 %copy-start.3 = (bf16[256,1152]{1,0:T(8,128)(2,1)S(1)}, bf16[256,1152]{1,0:T(8,128)(2,1)}, u32[]{:S(2)}) copy-start(bf16[256,1152]{1,0:T(8,128)(2,1)} %constant.18.clone.ph_ref) | copy-start | bytes 1769476
  5.8 0.9 %copy-start.4 = (bf16[384,256]{1,0:T(8,128)(2,1)S(1)}, bf16[384,256]{1,0:T(8,128)(2,1)}, u32[]{:S(2)}) copy-start(bf16[384,256]{1,0:T(8,128)(2,1)} %constant.21.clone.ml_ref) | copy-start | bytes 589828
  6.7 0.9 %copy-start.5 = (bf16[384,256]{1,0:T(8,128)(2,1)S(1)}, bf16[384,256]{1,0:T(8,128)(2,1)}, u32[]{:S(2)}) copy-start(bf16[384,256]{1,0:T(8,128)(2,1)} %constant.20.clone.mh_ref) | copy-start | bytes 589828
  7.7 0.8 %copy-start.6 = (f32[4,100,32]{1,2,0:T(8,128)S(1)}, f32[4,100,32]{1,2,0:T(8,128)}, u32[]{:S(2)}) copy-start(f32[4,100,32]{1,2,0:T(8,128)} %param.14) | copy-start | bytes 153604
  8.5 0.8 %copy-start.7 = (bf16[64,288]{1,0:T(8,128)(2,1)S(1)}, bf16[64,288]{1,0:T(8,128)(2,1)}, u32[]{:S(2)}) copy-start(bf16[64,288]{1,0:T(8,128)(2,1)} %constant.24.clone.fwd_ref) | copy-start | bytes 110596
  9.3 0.8 %copy-start.8 = (bf16[96,192]{1,0:T(8,128)(2,1)S(1)}, bf16[96,192]{1,0:T(8,128)(2,1)}, u32[]{:S(2)}) copy-start(bf16[96,192]{1,0:T(8,128)(2,1)} %constant.23.clone.slo_ref) | copy-start | bytes 110596
  10.1 0.8 %copy-start.9 = (bf16[96,192]{1,0:T(8,128)(2,1)S(1)}, bf16[96,192]{1,0:T(8,128)(2,1)}, u32[]{:S(2)}) copy-start(bf16[96,192]{1,0:T(8,128)(2,1)} %constant.22.clone.inv_ref) | copy-start | bytes 110596
  10.9 0.7 %copy-start.10 = (f32[100,32]{0,1:T(8,128)S(1)}, f32[100,32]{0,1:T(8,128)}, u32[]{:S(2)}) copy-start(f32[100,32]{0,1:T(8,128)} %param.15) | copy-start | bytes 38404

commit v2 on v1

--- a/solution.py
+++ b/solution.py
@@ -209,6 +209,7 @@
 WIDE = 256
 LANES = 128
 CHUNKS = 2
+TABLES = 9
 MESH = pl.DeviceIdType.MESH
 
 
@@ -254,12 +255,12 @@
                     edges[end, 1, slot, source + swapped, (3 - slot) * 32 + field * side + r] = sign
     edges = edges.reshape(4, 4 * WIDE, LANES).astype(jnp.bfloat16)
     return (
+        lanes,
         *halves(to_point),
-        *halves(to_mode),
         triple(inverse),
         triple(slope),
         triple(forward),
-        lanes,
+        *halves(to_mode),
         edges,
     )
 
@@ -287,8 +288,20 @@
     return jnp.concatenate([high, high, low], axis=0)
 
 
-def advance(n_plane, n_elem, flip_ref, vel_ref, geo_ref, jac_ref, ph_ref, pl_ref, mh_ref, ml_ref,
-            inv_ref, slo_ref, fwd_ref, lane_ref, edge_ref, adv_ref, svv_ref,
+def advance(n_plane, n_elem, flip_ref, *refs):
+    n_in = 3 + TABLES
+    sources, (adv_ref, svv_ref), held = refs[:n_in], refs[n_in : n_in + 2], refs[n_in + 2 : 2 * n_in + 2]
+    fetches = [
+        pltpu.make_async_copy(source, target, refs[-1].at[i])
+        for i, (source, target) in enumerate(zip(sources, held))
+    ]
+    for fetch in fetches:
+        fetch.start()
+    advance_block(n_plane, n_elem, fetches, flip_ref, *held, adv_ref, svv_ref, *refs[2 * n_in + 2 : -1])
+
+
+def advance_block(n_plane, n_elem, fetches, flip_ref, vel_ref, geo_ref, jac_ref, lane_ref, ph_ref,
+            pl_ref, inv_ref, slo_ref, fwd_ref, mh_ref, ml_ref, edge_ref, adv_ref, svv_ref,
             vel_s, pack_s, got_s, weight_s, energy_s, strength_s, point_s, hat_s, back_s, weak_s,
             edge_out, edge_in, out_s,
             send_a, recv_a, send_s, recv_s, send_b, recv_b, send_e, recv_e):
@@ -318,6 +331,7 @@
     def _():
         pl.semaphore_signal(barrier, inc=1, device_id=(block + 1, me), device_id_type=MESH)
 
+    fetches[0].wait()
     for field in range(3):
         vel_s[field * planes * elements : (field + 1) * planes * elements, 0:MODES] = vel_ref[field]
 
@@ -393,6 +407,8 @@
     for element in range(rows):
         got_s[me, element] = pack(me, element)
 
+    for fetch in fetches[1:]:
+        fetch.wait()
     start = pl.multiple_of(me * rows, 8)
     area = jac_ref[pl.ds(start, rows), :] * lane_ref[2:3, 0:POINTS]
     weight_s[...] = jnp.zeros_like(weight_s)
@@ -568,6 +584,7 @@
     vel = velocity.transpose(0, 1, 3, 2).reshape(3, planes * elements, MODES)
     geo = geometry.transpose(0, 2, 1)
     jac = jacobian.transpose(1, 0)
+    inputs = [vel, geo, jac, *tables]
     whole = pl.BlockSpec(memory_space=pltpu.VMEM)
     part = EY // CHUNKS
     flat = jax.ShapeDtypeStruct((3, planes * elements, MODES), jnp.float32)
@@ -577,9 +594,10 @@
     advection, svv = pl.pallas_call(
         functools.partial(advance, n_plane, n_elem),
         out_shape=(flat, flat),
-        in_specs=[pl.BlockSpec(memory_space=pltpu.SMEM)] + [whole] * (3 + len(tables)),
+        in_specs=[pl.BlockSpec(memory_space=pltpu.SMEM)] + [pl.BlockSpec(memory_space=pltpu.HBM)] * len(inputs),
         out_specs=(whole, whole),
-        scratch_shapes=[
+        scratch_shapes=[pltpu.VMEM(x.shape, x.dtype) for x in inputs]
+        + [
             pltpu.VMEM((3 * planes * elements, LANES), f32),
             pltpu.VMEM((others, EY, planes, WIDE), f32),
             pltpu.VMEM((n_plane, EY, planes, WIDE), f32),
@@ -601,11 +619,12 @@
             dma((others, CHUNKS)),
             dma((2,)),
             dma((2,)),
+            dma((len(inputs),)),
         ],
         compiler_params=pltpu.CompilerParams(
             collective_id=0, has_side_effects=True, vmem_limit_bytes=40 * 1024 * 1024
         ),
-    )(frame_flip, vel, geo, jac, *tables)
+    )(frame_flip, *inputs)
 
     def restore(x):
         return x.reshape(3, planes, elements, MODES).transpose(0, 1, 3, 2)

time: 37.8 us -> 39.7 us (1.050)
  Pallas kernels: 23.7 us -> 25 us
  local copies, waits for them, and re-layouts: 12.1 us -> 12.7 us
    pallas_call x1, Pallas kernels: 23.7 us -> 25 us  [kernel_body(): pl.pallas_call(functools.partial(advance, n_plane, n_elem), out_shape=(fl...]
    unnamed x26, local copies, waits for them, and re-layouts: 12.1 us -> 12.7 us
where the time goes in v2:
time: 39.7 us; the launch traced here: 39.1 us
  Pallas kernels  25 us (63%)
  local copies, waits for them, and re-layouts  12.7 us (32%)
  between operations  1.31 us (3%)
    pallas_call x1, Pallas kernels, kernel_body(): pl.pallas_call(functools.partial(advance, n_plane, n_elem), out_shape=(fl...  25 us
    unnamed x26, local copies, waits for them, and re-layouts  12.7 us

profile of v2, /device:TPU:0, one launch (start us, length us, event | category | flops | bytes accessed | tf_op | source)
XLA Modules:
  0.0 39.1 jit_solution(12152071243355973264)
XLA Ops:
  1.3 0.0 copy-start
  1.3 1.2 %copy-done = bf16[4,1024,128]{2,1,0:T(8,128)(2,1)S(1)} copy-done((bf16[4,1024,128]{2,1,0:T(8,128)(2,1)S(1)}, bf16[4,1024,128]{2,1,0:T(8,128)(2,1)}, u32[]{:S(2)}) %copy-start) | copy-done | bytes 1048600
  2.5 0.0 copy-start.1
  2.5 1.1 %copy-done.1 = f32[3,16,81,32]{2,3,1,0:T(8,128)S(1)} copy-done((f32[3,16,81,32]{2,3,1,0:T(8,128)S(1)}, f32[3,16,81,32]{2,3,1,0:T(8,128)}, u32[]{:S(2)}) %copy-start.1) | copy-done | bytes 497688
  3.6 0.0 copy-start.2
  3.6 1.1 %copy-done.2 = bf16[256,1152]{1,0:T(8,128)(2,1)S(1)} copy-done((bf16[256,1152]{1,0:T(8,128)(2,1)S(1)}, bf16[256,1152]{1,0:T(8,128)(2,1)}, u32[]{:S(2)}) %copy-start.2) | copy-done | bytes 589848
  4.7 0.0 copy-start.3
  4.7 1.1 %copy-done.3 = bf16[256,1152]{1,0:T(8,128)(2,1)S(1)} copy-done((bf16[256,1152]{1,0:T(8,128)(2,1)S(1)}, bf16[256,1152]{1,0:T(8,128)(2,1)}, u32[]{:S(2)}) %copy-start.3) | copy-done | bytes 589848
  5.8 0.0 copy-start.4
  5.8 0.9 %copy-done.4 = bf16[384,256]{1,0:T(8,128)(2,1)S(1)} copy-done((bf16[384,256]{1,0:T(8,128)(2,1)S(1)}, bf16[384,256]{1,0:T(8,128)(2,1)}, u32[]{:S(2)}) %copy-start.4) | copy-done | bytes 196632
  6.7 0.0 copy-start.5
  6.7 0.9 %copy-done.5 = bf16[384,256]{1,0:T(8,128)(2,1)S(1)} copy-done((bf16[384,256]{1,0:T(8,128)(2,1)S(1)}, bf16[384,256]{1,0:T(8,128)(2,1)}, u32[]{:S(2)}) %copy-start.5) | copy-done | bytes 196632
  7.6 0.0 copy-start.6
  7.6 0.8 %copy-done.6 = f32[4,100,32]{1,2,0:T(8,128)S(1)} copy-done((f32[4,100,32]{1,2,0:T(8,128)S(1)}, f32[4,100,32]{1,2,0:T(8,128)}, u32[]{:S(2)}) %copy-start.6) | copy-done | bytes 51224
  8.5 0.0 copy-start.7
  8.5 0.8 %copy-done.7 = bf16[64,288]{1,0:T(8,128)(2,1)S(1)} copy-done((bf16[64,288]{1,0:T(8,128)(2,1)S(1)}, bf16[64,288]{1,0:T(8,128)(2,1)}, u32[]{:S(2)}) %copy-start.7) | copy-done | bytes 36888
  9.3 0.0 copy-start.8
  9.3 0.8 %copy-done.8 = bf16[96,192]{1,0:T(8,128)(2,1)S(1)} copy-done((bf16[96,192]{1,0:T(8,128)(2,1)S(1)}, bf16[96,192]{1,0:T(8,128)(2,1)}, u32[]{:S(2)}) %copy-start.8) | copy-done | bytes 36888
  10.1 0.0 copy-start.9
  10.1 0.8 %copy-done.9 = bf16[96,192]{1,0:T(8,128)(2,1)S(1)} copy-done((bf16[96,192]{1,0:T(8,128)(2,1)S(1)}, bf16[96,192]{1,0:T(8,128)(2,1)}, u32[]{:S(2)}) %copy-start.9) | copy-done | bytes 36888
  10.9 0.0 copy-start.10
  10.9 0.7 %copy-done.10 = f32[100,32]{0,1:T(8,128)S(1)} copy-done((f32[100,32]{0,1:T(8,128)S(1)}, f32[100,32]{0,1:T(8,128)}, u32[]{:S(2)}) %copy-start.10) | copy-done | bytes 12824
  11.6 0.0 copy-start.11
  11.6 0.7 %copy-done.11 = f32[8,256]{1,0:T(8,128)S(1)} copy-done((f32[8,256]{1,0:T(8,128)S(1)}, f32[8,256]{1,0:T(8,128)}, u32[]{:S(2)}) %copy-start.11) | copy-done | bytes 8216
  12.3 25.0 %shard_map.140 = (f32[3,512,81]{2,1,0:T(8,128)S(1)}, f32[3,512,81]{2,1,0:T(8,128)S(1)}) custom-call(s32[1]{0:T(128)S(6)} %copy.17.flip_ref, f32[3,512,81]{2,1,0:T(8,128)S(1)} %bitcast.13, f32[4,32,100]{2,1,0:T(8,128)S(1)} %bitcast.14, f32[32,100]{1,0:T(8,128)S(1)} %bitcast.15, f32[8,256]{1,0:T(8,128)S(1)} %copy-done.11, bf16[256,1152]{1,0:T(8,128)(2,1)S(1)} %copy-done.3, ...), custom_call_target="tpu_custom_call" | custom-call | tf_op jit(solution)/shard_map/pallas_call | solution.py:594
  37.3 0.9 %copy.18 = f32[3,16,81,32]{2,3,1,0:T(8,128)} copy(f32[3,16,81,32]{2,3,1,0:T(8,128)S(1)} %bitcast.12) | data formatting | bytes 995328
  38.2 0.9 %copy.19 = f32[3,16,81,32]{2,3,1,0:T(8,128)} copy(f32[3,16,81,32]{2,3,1,0:T(8,128)S(1)} %bitcast.11) | data formatting | bytes 995328
Async XLA Ops:
  1.3 1.2 %copy-start = (bf16[4,1024,128]{2,1,0:T(8,128)(2,1)S(1)}, bf16[4,1024,128]{2,1,0:T(8,128)(2,1)}, u32[]{:S(2)}) copy-start(bf16[4,1024,128]{2,1,0:T(8,128)(2,1)} %constant.26.clone.refs_11_) | copy-start | bytes 3145732
  2.5 1.1 %copy-start.1 = (f32[3,16,81,32]{2,3,1,0:T(8,128)S(1)}, f32[3,16,81,32]{2,3,1,0:T(8,128)}, u32[]{:S(2)}) copy-start(f32[3,16,81,32]{2,3,1,0:T(8,128)} %param.13) | copy-start | bytes 1492996
  3.6 1.1 %copy-start.2 = (bf16[256,1152]{1,0:T(8,128)(2,1)S(1)}, bf16[256,1152]{1,0:T(8,128)(2,1)}, u32[]{:S(2)}) copy-start(bf16[256,1152]{1,0:T(8,128)(2,1)} %constant.20.clone.refs_5_) | copy-start | bytes 1769476
  4.7 1.1 %copy-start.3 = (bf16[256,1152]{1,0:T(8,128)(2,1)S(1)}, bf16[256,1152]{1,0:T(8,128)(2,1)}, u32[]{:S(2)}) copy-start(bf16[256,1152]{1,0:T(8,128)(2,1)} %constant.19.clone.refs_4_) | copy-start | bytes 1769476
  5.8 0.9 %copy-start.4 = (bf16[384,256]{1,0:T(8,128)(2,1)S(1)}, bf16[384,256]{1,0:T(8,128)(2,1)}, u32[]{:S(2)}) copy-start(bf16[384,256]{1,0:T(8,128)(2,1)} %constant.25.clone.refs_10_) | copy-start | bytes 589828
  6.7 0.9 %copy-start.5 = (bf16[384,256]{1,0:T(8,128)(2,1)S(1)}, bf16[384,256]{1,0:T(8,128)(2,1)}, u32[]{:S(2)}) copy-start(bf16[384,256]{1,0:T(8,128)(2,1)} %constant.24.clone.refs_9_) | copy-start | bytes 589828
  7.6 0.8 %copy-start.6 = (f32[4,100,32]{1,2,0:T(8,128)S(1)}, f32[4,100,32]{1,2,0:T(8,128)}, u32[]{:S(2)}) copy-start(f32[4,100,32]{1,2,0:T(8,128)} %param.14) | copy-start | bytes 153604
  8.5 0.8 %copy-start.7 = (bf16[64,288]{1,0:T(8,128)(2,1)S(1)}, bf16[64,288]{1,0:T(8,128)(2,1)}, u32[]{:S(2)}) copy-start(bf16[64,288]{1,0:T(8,128)(2,1)} %constant.23.clone.refs_8_) | copy-start | bytes 110596
  9.3 0.8 %copy-start.8 = (bf16[96,192]{1,0:T(8,128)(2,1)S(1)}, bf16[96,192]{1,0:T(8,128)(2,1)}, u32[]{:S(2)}) copy-start(bf16[96,192]{1,0:T(8,128)(2,1)} %constant.22.clone.refs_7_) | copy-start | bytes 110596
  10.1 0.8 %copy-start.9 = (bf16[96,192]{1,0:T(8,128)(2,1)S(1)}, bf16[96,192]{1,0:T(8,128)(2,1)}, u32[]{:S(2)}) copy-start(bf16[96,192]{1,0:T(8,128)(2,1)} %constant.21.clone.refs_6_) | copy-start | bytes 110596
  10.9 0.7 %copy-start.10 = (f32[100,32]{0,1:T(8,128)S(1)}, f32[100,32]{0,1:T(8,128)}, u32[]{:S(2)}) copy-start(f32[100,32]{0,1:T(8,128)} %param.15) | copy-start | bytes 38404
  11.6 0.7 %copy-start.11 = (f32[8,256]{1,0:T(8,128)S(1)}, f32[8,256]{1,0:T(8,128)}, u32[]{:S(2)}) copy-start(f32[8,256]{1,0:T(8,128)} %constant.18.clone.refs_3_) | copy-start | bytes 24580

commit v3 on v2

--- a/solution.py
+++ b/solution.py
@@ -208,7 +208,7 @@
 FINE = 3 * NZ // 2
 WIDE = 256
 LANES = 128
-CHUNKS = 2
+CHUNKS = 4
 TABLES = 9
 MESH = pl.DeviceIdType.MESH
 
@@ -290,20 +290,20 @@
 
 def advance(n_plane, n_elem, flip_ref, *refs):
     n_in = 3 + TABLES
-    sources, (adv_ref, svv_ref), held = refs[:n_in], refs[n_in : n_in + 2], refs[n_in + 2 : 2 * n_in + 2]
+    sources, (joined_ref, sense_ref), held = refs[:n_in], refs[n_in : n_in + 2], refs[n_in + 2 : 2 * n_in + 2]
     fetches = [
         pltpu.make_async_copy(source, target, refs[-1].at[i])
         for i, (source, target) in enumerate(zip(sources, held))
     ]
     for fetch in fetches:
         fetch.start()
-    advance_block(n_plane, n_elem, fetches, flip_ref, *held, adv_ref, svv_ref, *refs[2 * n_in + 2 : -1])
+    advance_block(n_plane, n_elem, fetches, flip_ref, *held, joined_ref, sense_ref, *refs[2 * n_in + 2 : -1])
 
 
 def advance_block(n_plane, n_elem, fetches, flip_ref, vel_ref, geo_ref, jac_ref, lane_ref, ph_ref,
-            pl_ref, inv_ref, slo_ref, fwd_ref, mh_ref, ml_ref, edge_ref, adv_ref, svv_ref,
+            pl_ref, inv_ref, slo_ref, fwd_ref, mh_ref, ml_ref, edge_ref, joined_ref, sense_ref,
             vel_s, pack_s, got_s, weight_s, energy_s, strength_s, point_s, hat_s, back_s, weak_s,
-            edge_out, edge_in, out_s,
+            edge_out, edge_in,
             send_a, recv_a, send_s, recv_s, send_b, recv_b, send_e, recv_e):
     block = lax.axis_index("elem")
     me = lax.axis_index("plane")
@@ -470,12 +470,7 @@
 
     for i in range(len(offsets)):
         strength_copy(i).wait_recv()
-    for column in range(columns):
-        factor = -strength_s[column] * lane_ref[1:2, 0:LANES]
-        for field in range(3):
-            for j in range(planes):
-                at = slice(j * elements + column * rows, j * elements + (column + 1) * rows)
-                svv_ref[field, at, :] = vel_ref[field, at, :] * factor[:, 0:MODES]
+    sense_ref[...] = strength_s[0:n_plane]
 
     for chunk in range(CHUNKS):
         for i in range(len(offsets)):
@@ -506,8 +501,6 @@
     inside = wide < 3 * MODES
     is_left = inside & (lax.rem(wide, MODES) < side)
     is_right = inside & (lax.rem(wide, MODES) >= side) & (lax.rem(wide, MODES) < 2 * side)
-    is_bottom = inside & (lax.rem(wide, side) == 0)
-    is_top = inside & (lax.rem(wide, side) == 1)
 
     for row in range(rows):
         strip = [weak_s[column, row] for column in range(columns)]
@@ -544,24 +537,7 @@
             for s in range(4):
                 got_s[column, 4 * half + s] += spread[:, s * WIDE : (s + 1) * WIDE]
 
-    for column in range(columns):
-        strip = [got_s[column, row] for row in range(rows)]
-        for row in range(rows):
-            total = strip[row]
-            if row > 0:
-                total = total + jnp.where(is_bottom, pltpu.roll(strip[row - 1], WIDE - 1, 1), 0.0)
-            if row < rows - 1:
-                total = total + jnp.where(is_top, pltpu.roll(strip[row + 1], 1, 1), 0.0)
-            fields = (
-                total[:, 0:LANES],
-                pltpu.roll(total, WIDE - MODES, 1)[:, 0:LANES],
-                pltpu.roll(total, WIDE - 2 * MODES, 1)[:, 0:LANES],
-            )
-            for field in range(3):
-                base = field * planes * elements + column * rows + row
-                out_s[pl.ds(base, planes, stride=elements), :] = fields[field]
-    for field in range(3):
-        adv_ref[field] = out_s[field * planes * elements : (field + 1) * planes * elements, 0:MODES]
+    joined_ref[...] = got_s[...]
 
     for i in range(len(offsets)):
         strength_copy(i).wait_send()
@@ -576,6 +552,34 @@
     @pl.when(has_next)
     def _():
         edge_copy(1, block + 1).wait_send()
+
+
+def finish(joined_ref, sense_ref, vel_ref, lane_ref, adv_ref, svv_ref, out_s):
+    planes = joined_ref.shape[2]
+    side = P_SIZE + 1
+    wide = lax.broadcasted_iota(jnp.int32, (planes, WIDE), 1)
+    inside = wide < 3 * MODES
+    is_bottom = inside & (lax.rem(wide, side) == 0)
+    is_top = inside & (lax.rem(wide, side) == 1)
+    factor = -sense_ref[0] * lane_ref[1:2, 0:LANES]
+    svv_ref[...] = vel_ref[...] * factor[:, 0:MODES]
+    strip = [joined_ref[0, row] for row in range(EY)]
+    for row in range(EY):
+        total = strip[row]
+        if row > 0:
+            total = total + jnp.where(is_bottom, pltpu.roll(strip[row - 1], WIDE - 1, 1), 0.0)
+        if row < EY - 1:
+            total = total + jnp.where(is_top, pltpu.roll(strip[row + 1], 1, 1), 0.0)
+        fields = (
+            total[:, 0:LANES],
+            pltpu.roll(total, WIDE - MODES, 1)[:, 0:LANES],
+            pltpu.roll(total, WIDE - 2 * MODES, 1)[:, 0:LANES],
+        )
+        for field in range(3):
+            out_s[pl.ds(field * planes * EY + row, planes, stride=EY), :] = fields[field]
+    for field in range(3):
+        block = out_s[field * planes * EY : (field + 1) * planes * EY, 0:MODES]
+        adv_ref[field] = block.reshape(planes, EY, MODES)
 
 
 def kernel_body(n_plane, n_elem, velocity, geometry, jacobian, frame_flip):
@@ -587,13 +591,15 @@
     inputs = [vel, geo, jac, *tables]
     whole = pl.BlockSpec(memory_space=pltpu.VMEM)
     part = EY // CHUNKS
-    flat = jax.ShapeDtypeStruct((3, planes * elements, MODES), jnp.float32)
     f32 = jnp.float32
     dma = pltpu.SemaphoreType.DMA
     others = n_plane - 1
-    advection, svv = pl.pallas_call(
+    joined, sense = pl.pallas_call(
         functools.partial(advance, n_plane, n_elem),
-        out_shape=(flat, flat),
+        out_shape=(
+            jax.ShapeDtypeStruct((n_plane, EY, planes, WIDE), f32),
+            jax.ShapeDtypeStruct((n_plane, EY, LANES), f32),
+        ),
         in_specs=[pl.BlockSpec(memory_space=pltpu.SMEM)] + [pl.BlockSpec(memory_space=pltpu.HBM)] * len(inputs),
         out_specs=(whole, whole),
         scratch_shapes=[pltpu.VMEM(x.shape, x.dtype) for x in inputs]
@@ -610,7 +616,6 @@
             pltpu.VMEM((n_plane, EY, planes, WIDE), f32),
             pltpu.VMEM((2, 2, planes, LANES), f32),
             pltpu.VMEM((2, 2, planes, LANES), f32),
-            pltpu.VMEM((3 * planes * elements, LANES), f32),
             dma((others, CHUNKS)),
             dma((others, CHUNKS)),
             dma((others,)),
@@ -622,14 +627,27 @@
             dma((len(inputs),)),
         ],
         compiler_params=pltpu.CompilerParams(
-            collective_id=0, has_side_effects=True, vmem_limit_bytes=40 * 1024 * 1024
+            collective_id=0, has_side_effects=True, vmem_limit_bytes=61 * 1024 * 1024
         ),
     )(frame_flip, *inputs)
 
-    def restore(x):
-        return x.reshape(3, planes, elements, MODES).transpose(0, 1, 3, 2)
-
-    return restore(advection), restore(svv)
+    slab = pl.BlockSpec((3, planes, EY, MODES), lambda c: (0, 0, c, 0))
+    full = jax.ShapeDtypeStruct((3, planes, elements, MODES), f32)
+    advection, svv = pl.pallas_call(
+        finish,
+        out_shape=(full, full),
+        grid=(n_plane,),
+        in_specs=[
+            pl.BlockSpec((1, EY, planes, WIDE), lambda c: (c, 0, 0, 0)),
+            pl.BlockSpec((1, EY, LANES), lambda c: (c, 0, 0)),
+            slab,
+            pl.BlockSpec((8, WIDE), lambda c: (0, 0)),
+        ],
+        out_specs=(slab, slab),
+        scratch_shapes=[pltpu.VMEM((3 * planes * EY, LANES), f32)],
+        compiler_params=pltpu.CompilerParams(vmem_limit_bytes=61 * 1024 * 1024),
+    )(joined, sense, velocity.transpose(0, 1, 3, 2), tables[0])
+    return advection.transpose(0, 1, 3, 2), svv.transpose(0, 1, 3, 2)
 
 
 def body(velocity, geometry, jacobian, frame_flip):

time: 39.7 us -> 27.7 us (0.70)
  local copies, waits for them, and re-layouts: 12.7 us -> 0 us
  Pallas kernels: 25 us -> 26.2 us
    unnamed x26 -> x0, local copies, waits for them, and re-layouts: 12.7 us -> none
    pallas_call x1 -> x2, Pallas kernels: 25 us -> 26.2 us  [the longest x1 22.3 us: kernel_body(): pl.pallas_call(functools.partial(advance, n_plane, n_elem), out_shape=(ja...]
where the time goes in v3:
time: 27.7 us; the launch traced here: 27.5 us
  Pallas kernels  26.2 us (95%)
  between operations  1.28 us (5%)
    pallas_call x1, Pallas kernels, kernel_body(): pl.pallas_call(functools.partial(advance, n_plane, n_elem), out_shape=(ja...  22.3 us
    pallas_call x1, Pallas kernels, kernel_body(): pl.pallas_call(finish, out_shape=(full, full), grid=(n_plane,), in_specs=...  3.94 us

profile of v3, /device:TPU:0, one launch (start us, length us, event | category | flops | bytes accessed | tf_op | source)
XLA Modules:
  0.0 27.5 jit_solution(1440820947868333543)
XLA Ops:
  1.3 22.3 %shard_map.140 = (f32[4,8,16,256]{3,2,1,0:T(8,128)}, f32[4,8,128]{2,1,0:T(8,128)}) custom-call(s32[1]{0:T(128)S(6)} %copy.15.flip_ref, f32[3,512,81]{2,1,0:T(8,128)} %bitcast.7, f32[4,32,100]{2,1,0:T(8,128)} %bitcast.9, f32[32,100]{1,0:T(8,128)} %bitcast.10, f32[8,256]{1,0:T(8,128)} %constant.18.clone.refs_3_.lane_ref, ...), custom_call_target="tpu_custom_call" | custom-call | tf_op jit(solution)/shard_map/pallas_call | solution.py:597
  23.5 3.9 %shard_map.141 = (f32[3,16,32,81]{3,2,1,0:T(8,128)}, f32[3,16,32,81]{3,2,1,0:T(8,128)}) custom-call(f32[4,8,16,256]{3,2,1,0:T(8,128)} %get-tuple-element.6.joined_ref, f32[4,8,128]{2,1,0:T(8,128)} %get-tuple-element.7.sense_ref, f32[3,16,32,81]{3,2,1,0:T(8,128)} %bitcast.8, f32[8,256]{1,0:T(8,128)} %constant.18.clone.refs_3_.lane_ref), custom_call_target="tpu_custom_call" | custom-call | tf_op jit(solution)/shard_map/pallas_call | solution.py:636

commit v4 on v3

--- a/solution.py
+++ b/solution.py
@@ -242,6 +242,11 @@
     lanes[0, : 3 * MODES] = np.tile(tail, 3)
     lanes[1, :MODES] = svv
     lanes[2, :POINTS] = weights
+    mode = np.arange(3 * MODES)
+    lanes[3, : 3 * MODES] = mode % MODES // (P_SIZE + 1) == 0
+    lanes[4, : 3 * MODES] = mode % MODES // (P_SIZE + 1) == 1
+    lanes[5, : 3 * MODES] = mode % (P_SIZE + 1) == 0
+    lanes[6, : 3 * MODES] = mode % (P_SIZE + 1) == 1
     edges = np.zeros((2, 2, 4, WIDE, LANES), np.float32)
     side = P_SIZE + 1
     for end in range(2):
@@ -394,20 +399,25 @@
             device_id_type=MESH,
         )
 
-    for chunk in range(CHUNKS):
+    pl.semaphore_wait(
+        barrier, len(offsets) + has_prev.astype(jnp.int32) + has_next.astype(jnp.int32)
+    )
+
+    def send_chunk(chunk, carry):
         for i, offset in enumerate(offsets):
-            target = peer(offset)
-            for element in range(chunk * part, (chunk + 1) * part):
-                pack_s[i, element] = pack(target, element)
-            if chunk == 0 and i == 0:
-                pl.semaphore_wait(
-                    barrier, len(offsets) + has_prev.astype(jnp.int32) + has_next.astype(jnp.int32)
-                )
+            for local in range(part):
+                pack_s[i, chunk * part + local] = pack(peer(offset), chunk * part + local)
             forward_copy(i, chunk).start()
-    for element in range(rows):
+        return carry
+
+    lax.fori_loop(0, CHUNKS, send_chunk, 0)
+
+    def keep_own(element, carry):
         got_s[me, element] = pack(me, element)
-
-    for fetch in fetches[1:]:
+        return carry
+
+    lax.fori_loop(0, rows, keep_own, 0)
+    for fetch in fetches[1:-1]:
         fetch.wait()
     start = pl.multiple_of(me * rows, 8)
     area = jac_ref[pl.ds(start, rows), :] * lane_ref[2:3, 0:POINTS]
@@ -416,34 +426,21 @@
         weight_s[i, :, 0:POINTS] = geo_ref[i, pl.ds(start, rows), :] * area
     weight_s[4, :, 0:POINTS] = area
 
-    for chunk in range(CHUNKS):
+    def work(chunk, carry):
         for i in range(len(offsets)):
             forward_copy(i, chunk).wait_recv()
-        span = slice(chunk * part, (chunk + 1) * part)
         x = jnp.concatenate(
-            [got_s[source, element] for element in range(chunk * part, (chunk + 1) * part)
+            [got_s[source, chunk * part + local] for local in range(part)
              for source in range(n_plane)], axis=0)
-        energy_s[span, :] = jnp.sum((x * x).reshape(part, NZ, WIDE), axis=1)
+        energy_s[chunk] = jnp.sum((x * x).reshape(part, NZ, WIDE), axis=1)
         point_s[...] = dot3(x, ph_ref[...], pl_ref[...])
-        if chunk == CHUNKS - 1:
-            squares = energy_s[...]
-            tail_energy = jnp.sum(squares * lane_ref[0:1, :], axis=1, keepdims=True)
-            all_energy = jnp.sum(squares, axis=1, keepdims=True)
-            log_share = jnp.log((tail_energy + energy_floor) / (all_energy + energy_floor))
-            ramp = (log_share - sensor_centre) / sensor_width
-            strength = svv_peak / (1.0 + jnp.exp(-ramp))
-            strength_s[n_plane] = jnp.broadcast_to(strength, (rows, LANES))
-            strength_s[me] = jnp.broadcast_to(strength, (rows, LANES))
-            for i in range(len(offsets)):
-                strength_copy(i).start()
-
         for local in range(part):
             element = chunk * part + local
             here = slice(local * NZ, (local + 1) * NZ)
             u = point_s[here, 0:LANES]
             v = point_s[here, LANES : 2 * LANES]
             w = point_s[here, 2 * LANES : 3 * LANES]
-            g = [weight_s[i, element : element + 1, :] for i in range(5)]
+            g = [weight_s[i, pl.ds(element, 1), :] for i in range(5)]
             carriers = jnp.concatenate([g[0] * u + g[2] * v, g[1] * u + g[3] * v, g[4] * w], axis=1)
             speeds = dot(inv_ref[...], stacked_halves(carriers))
             slopes = dot(inv_ref[...], stacked_halves(point_s[here, 3 * LANES :]))
@@ -467,6 +464,20 @@
             back_copy(i, chunk).start()
         for local in range(part):
             weak_s[me, chunk * part + local] = back_s[me, chunk * part + local]
+        return carry
+
+    lax.fori_loop(0, CHUNKS, work, 0)
+    squares = jnp.concatenate([energy_s[c] for c in range(CHUNKS)], axis=0)
+    tail_energy = jnp.sum(squares * lane_ref[0:1, :], axis=1, keepdims=True)
+    all_energy = jnp.sum(squares, axis=1, keepdims=True)
+    log_share = jnp.log((tail_energy + energy_floor) / (all_energy + energy_floor))
+    ramp = (log_share - sensor_centre) / sensor_width
+    strength = svv_peak / (1.0 + jnp.exp(-ramp))
+    strength_s[n_plane] = jnp.broadcast_to(strength, (rows, LANES))
+    strength_s[me] = jnp.broadcast_to(strength, (rows, LANES))
+    for i in range(len(offsets)):
+        strength_copy(i).start()
+
 
     for i in range(len(offsets)):
         strength_copy(i).wait_recv()
@@ -476,6 +487,7 @@
         for i in range(len(offsets)):
             back_copy(i, chunk).wait_recv()
 
+    fetches[-1].wait()
     flipped = flip_ref[0] == 1
     turn = jnp.where(flipped, 1, 0)
     for i, column in ((0, 0), (1, columns - 1)):
@@ -496,13 +508,11 @@
     def _():
         edge_copy(1, block + 1).start()
 
-    wide = lax.broadcasted_iota(jnp.int32, (planes, WIDE), 1)
     side = P_SIZE + 1
-    inside = wide < 3 * MODES
-    is_left = inside & (lax.rem(wide, MODES) < side)
-    is_right = inside & (lax.rem(wide, MODES) >= side) & (lax.rem(wide, MODES) < 2 * side)
-
-    for row in range(rows):
+    is_left = lane_ref[3:4, :] > 0.0
+    is_right = lane_ref[4:5, :] > 0.0
+
+    def join_row(row, carry):
         strip = [weak_s[column, row] for column in range(columns)]
         for column in range(columns):
             total = strip[column]
@@ -511,6 +521,9 @@
             if column < columns - 1:
                 total = total + jnp.where(is_right, pltpu.roll(strip[column + 1], side, 1), 0.0)
             got_s[column, row] = total
+        return carry
+
+    lax.fori_loop(0, rows, join_row, 0)
 
     @pl.when(has_next)
     def _():
@@ -556,11 +569,8 @@
 
 def finish(joined_ref, sense_ref, vel_ref, lane_ref, adv_ref, svv_ref, out_s):
     planes = joined_ref.shape[2]
-    side = P_SIZE + 1
-    wide = lax.broadcasted_iota(jnp.int32, (planes, WIDE), 1)
-    inside = wide < 3 * MODES
-    is_bottom = inside & (lax.rem(wide, side) == 0)
-    is_top = inside & (lax.rem(wide, side) == 1)
+    is_bottom = lane_ref[5:6, :] > 0.0
+    is_top = lane_ref[6:7, :] > 0.0
     factor = -sense_ref[0] * lane_ref[1:2, 0:LANES]
     svv_ref[...] = vel_ref[...] * factor[:, 0:MODES]
     strip = [joined_ref[0, row] for row in range(EY)]
@@ -608,7 +618,7 @@
             pltpu.VMEM((others, EY, planes, WIDE), f32),
             pltpu.VMEM((n_plane, EY, planes, WIDE), f32),
             pltpu.VMEM((5, EY, LANES), f32),
-            pltpu.VMEM((EY, WIDE), f32),
+            pltpu.VMEM((CHUNKS, part, WIDE), f32),
             pltpu.VMEM((n_plane + 1, EY, LANES), f32),
             pltpu.VMEM((part * NZ, 9 * LANES), f32),
             pltpu.VMEM((part * NZ, 3 * LANES), f32),

time: 27.7 us -> 27.6 us (level)
  no operation moved by 1% of the time
where the time goes in v4:
time: 27.6 us; the launch traced here: 27.4 us
  Pallas kernels  26.2 us (95%)
  between operations  1.28 us (5%)
    pallas_call x1, Pallas kernels, kernel_body(): pl.pallas_call(functools.partial(advance, n_plane, n_elem), out_shape=(ja...  22.2 us
    pallas_call x1, Pallas kernels, kernel_body(): pl.pallas_call(finish, out_shape=(full, full), grid=(n_plane,), in_specs=...  3.94 us

profile of v4, /device:TPU:0, one launch (start us, length us, event | category | flops | bytes accessed | tf_op | source)
XLA Modules:
  0.0 27.4 jit_solution(11508631850097923716)
XLA Ops:
  1.3 22.2 %shard_map.140 = (f32[4,8,16,256]{3,2,1,0:T(8,128)}, f32[4,8,128]{2,1,0:T(8,128)}) custom-call(s32[1]{0:T(128)S(6)} %copy.15.flip_ref, f32[3,512,81]{2,1,0:T(8,128)} %bitcast.7, f32[4,32,100]{2,1,0:T(8,128)} %bitcast.9, f32[32,100]{1,0:T(8,128)} %bitcast.10, f32[8,256]{1,0:T(8,128)} %constant.18.clone.refs_3_.lane_ref, ...), custom_call_target="tpu_custom_call" | custom-call | tf_op jit(solution)/shard_map/pallas_call | solution.py:607
  23.5 3.9 %shard_map.141 = (f32[3,16,32,81]{3,2,1,0:T(8,128)}, f32[3,16,32,81]{3,2,1,0:T(8,128)}) custom-call(f32[4,8,16,256]{3,2,1,0:T(8,128)} %get-tuple-element.6.joined_ref, f32[4,8,128]{2,1,0:T(8,128)} %get-tuple-element.7.sense_ref, f32[3,16,32,81]{3,2,1,0:T(8,128)} %bitcast.8, f32[8,256]{1,0:T(8,128)} %constant.18.clone.refs_3_.lane_ref), custom_call_target="tpu_custom_call" | custom-call | tf_op jit(solution)/shard_map/pallas_call | solution.py:646
